TPU v7x, 256 devices: a whole 4x4x8 slice. The times are simulated.
256 devices in a mesh: row: 32 (over z, y_hi, core), col: 8 (over x, y_lo).
Axes of the slice: x: 4, y: 4 (y_hi: 2, y_lo: 2; y = y_hi * 2 + y_lo), z: 8, core: 2. Of those that a mesh axis runs over, the one named last changes fastest.
Arguments:
- start_prev: float32 [512, 1024, 128], P('row', 'col'), may hold values from -6 to 6
- start_cur: float32 [512, 1024, 128], P('row', 'col'), may hold values from -6 to 6
- adj_prev: float32 [512, 1024, 128], P('row', 'col'), may hold values from -6 to 6
- adj_cur: float32 [512, 1024, 128], P('row', 'col'), may hold values from -6 to 6
- material: int32 [512, 1024, 128], P('row', 'col'), may hold values from 0 to 7
- speed_sq: float32 [8], replicated, may hold values from 0.08 to 0.32
- admittance: float32 [8, 2048], P('col', 'row'), may hold values from 0.2 to 2
- bound_cell: int32 [32, 16384], P('row', 'col'), may hold values from -1 to 262143, as said below
- bound_patch: int32 [32, 16384], P('row', 'col'), may hold values from -1 to 2047, as said below
Outputs:
- grad_prev: float32 [512, 1024, 128], P('row', 'col')
- grad_cur: float32 [512, 1024, 128], P('row', 'col')
- patch_grad: float32 [8, 2048], P('col', 'row')
Inputs may be any that keep to these rules, and one draw needn't show every extreme that they name: `bound_cell`: in each block's 2048 entries the live ones come first, in rising order and distinct, as flat indices x * 128 * 128 + y * 128 + z of cells inside that block; the rest are -1. Every block has at least 1024 live entries, and some block has all 2048. `bound_patch`: -1 exactly where bound_cell is -1.
All inputs are finite; a program needn't handle non-finite values.
Results may differ from a plain program's by a relative error of at most 0.00002.
Values sent between devices are 32-bit elements; how exact they have to be, the bound alone decides.
A program may use at most 64 MiB of HBM per device.

v0:
```python
import jax
import jax.numpy as jnp
from jax import lax
from jax.sharding import PartitionSpec as P

STEPS = 4


def extended(block, sides, width):
    for axis, dim in sides:
        count = lax.axis_size(axis)
        forward = [(i, i + 1) for i in range(count - 1)]
        backward = [(target, source) for source, target in forward]
        low = lax.ppermute(
            lax.slice_in_dim(block, block.shape[dim] - width, None, axis=dim), axis, forward
        )
        high = lax.ppermute(lax.slice_in_dim(block, 0, width, axis=dim), axis, backward)
        block = jnp.concatenate([low, block, high], axis=dim)
    return block


def beside_all(padded):
    total = padded[2:, 1:-1, 1:-1] + padded[:-2, 1:-1, 1:-1]
    total = total + padded[1:-1, 2:, 1:-1] + padded[1:-1, :-2, 1:-1]
    total = total + padded[1:-1, 1:-1, 2:] + padded[1:-1, 1:-1, :-2]
    return total


def sweep(start_prev, start_cur, adj_prev, adj_cur, c2, gamma, apply_laplace):
    states = [start_prev, start_cur]
    for step in range(STEPS):
        prev = states[-2]
        cur = states[-1]
        drive = 2.0 * cur + c2 * apply_laplace(cur)
        states.append((drive - (1.0 - gamma) * prev) / (1.0 + gamma))
    m_low = adj_prev
    m_high = adj_cur
    terms = []
    for level in range(STEPS, 0, -1):
        weight = m_high / (1.0 + gamma)
        terms.append(weight * (states[level - 1] - states[level + 1]))
        m_new = m_low + 2.0 * weight + apply_laplace(c2 * weight)
        m_low = -(1.0 - gamma) * weight
        m_high = m_new
    return (m_low, m_high, terms)


def local(
    start_prev,
    start_cur,
    adj_prev,
    adj_cur,
    material,
    speed_sq,
    admittance,
    bound_cell,
    bound_patch,
):
    c2 = jnp.zeros(material.shape, jnp.float32)
    for which in range(speed_sq.shape[0]):
        c2 = jnp.where(material == which, speed_sq[which], c2)
    strip = lax.all_gather(admittance, "row", axis=1, tiled=True)
    cells = bound_cell[0]
    patches = bound_patch[0]
    live = cells >= 0
    safe_cell = jnp.maximum(cells, 0)
    safe_patch = jnp.maximum(patches, 0)
    slot_gamma = jnp.where(live, 0.25 * strip[0][safe_patch], jnp.float32(0.0))
    gamma = jnp.zeros((c2.size,), jnp.float32).at[safe_cell].add(slot_gamma).reshape(c2.shape)

    def halo_laplace(field):
        padded = extended(field, (("row", 0), ("col", 1)), 1)
        padded = jnp.pad(padded, ((0, 0), (0, 0), (1, 1)))
        return beside_all(padded) - 6.0 * field

    grad_prev, grad_cur, terms = sweep(
        start_prev, start_cur, adj_prev, adj_cur, c2, gamma, halo_laplace
    )
    grad_gamma = terms[0]
    for extra in terms[1:]:
        grad_gamma = grad_gamma + extra
    values = jnp.where(live, 0.25 * grad_gamma.reshape(-1)[safe_cell], jnp.float32(0.0))
    partial_sums = jnp.zeros((strip.shape[1],), jnp.float32).at[safe_patch].add(values)
    patch_grad = lax.psum_scatter(partial_sums[None, :], "row", scatter_dimension=1, tiled=True)
    return (grad_prev, grad_cur, patch_grad)


def solution(mesh):
    placed = (
        P("row", "col", None),
        P("row", "col", None),
        P("row", "col", None),
        P("row", "col", None),
        P("row", "col", None),
        P(),
        P("col", "row"),
        P("row", "col"),
        P("row", "col"),
    )
    return jax.shard_map(
        local,
        mesh=mesh,
        in_specs=placed,
        out_specs=(P("row", "col", None), P("row", "col", None), P("col", "row")),
        check_vma=False,
    )
```

profile of v0, /device:TPU:1, one launch (start us, length us, event | category | flops | bytes accessed | tf_op | source)
XLA Modules:
  0.0 446.9 jit_solution(11983827876960413499)
XLA Ops:
  8.1 5.1 %collective-permute-start.16 = (f32[1,128,128]{2,1,0:T(8,128)S(1)}, f32[1,128,128]{2,1,0:T(8,128)S(1)}, u32[]{:S(2)}, u32[]{:S(2)}) collective-permute-start(f32[1,128,128]{2,1,0:T(8,128)S(1)} %get-tuple-element.45), channel_id=1, source_target_pairs={{8,0},{16,8},{24,16},{32,24},{40,32},{48,40},{56,48},{64,56},{72,6... | collective-permute-start | bytes 196616 | tf_op jit(solution)/shard_map/ppermute | solution.py:17
  13.3 3.0 collective-permute-start.17
  22.8 66.3 %all-reduce.8 = f32[2048]{0:T(1024)S(1)} all-reduce(f32[2048]{0:T(1024)S(1)} %bitcast_dynamic-update-slice_fusion), channel_id=1, replica_groups=mesh['row'=32,'col'=8] {'row'}, use_global_device_ids=true, to_apply=%add.8 | all-reduce | flops 2048 | bytes 16384 | tf_op jit(solution)/shard_map/squeeze | solution.py:68
  89.0 11.8 %gather_fusion = f32[2048]{0:T(1024)S(1)} fusion(f32[2048]{0:T(1024)S(1)} %all-reduce.8, s32[2048]{0:T(1024)S(1)} %broadcast_clamp_fusion.1), kind=kCustom, calls=%fused_computation | custom fusion | bytes 24576 | tf_op jit(solution)/shard_map/gather | solution.py:68
  100.9 14.4 %scatter_custom_fusion = f32[262144]{0:T(1024)S(1)} fusion(s32[2048]{0:T(1024)S(1)} %bitcast.38, f32[2048]{0:T(1024)S(1)} %multiply_select_fusion.1, f32[]{:T(128)} %constant.14.clone.1), kind=kCustom, calls=%fused_computation.175 | custom fusion | flops 2048 | bytes 1048580 | tf_op jit(solution)/shard_map/scatter-add | solution.py:69
  115.4 7.0 %fusion.68 = (f32[16,128,128]{2,1,0:T(8,128)S(1)}, f32[16,128,128]{2,1,0:T(8,128)S(1)}) fusion(f32[]{:T(128)} %bitcast.15, s32[16,128,128]{2,1,0:T(8,128)S(1)} %copy-done, f32[]{:T(128)} %bitcast.14, f32[]{:T(128)} %bitcast.13, f32[]{:T(128)} %bitcast.12, f32[]{:T(128)} %bitcast.11, f32[]{:T(128)} %bitcast.10, f32[]{:T(128)} %bitcast.9, f32[]{:T(128)} %bitcast.8, ...), kind=kLoop, calls=%fused_computation.216 | loop fusion | flops 4718592 | bytes 5242912 | tf_op jit(solution)/shard_map/mul | solution.py:42
  122.4 3.6 collective-permute-start.1
  126.0 4.0 collective-permute-start
  134.1 4.9 %collective-permute-start.3 = (f32[18,1,128]{2,1,0:T(1,128)S(1)}, f32[18,1,128]{2,1,0:T(1,128)S(1)}, u32[]{:S(2)}, u32[]{:S(2)}) collective-permute-start(f32[18,1,128]{2,1,0:T(1,128)S(1)} %get-tuple-element.19), channel_id=1, source_target_pairs={{0,1},{1,2},{2,3},{3,4},{4,5},{5,6},{6,7},{8,9},{9,10},{10,11},{11... | collective-permute-start | bytes 27656 | tf_op jit(solution)/shard_map/ppermute | solution.py:14
  141.1 7.4 %fusion.34 = f32[16,128,128]{2,1,0:T(8,128)S(1)} fusion(f32[16,128,128]{2,1,0:T(8,128)S(1)} %bitcast.21, f32[18,130,130]{2,1,0:T(8,128)S(1)} %select_maximum_fusion.12, f32[18,128,128]{2,1,0:T(8,128)S(1)} %constant_dynamic-update-slice_fusion, f32[18,1,128]{2,1,0:T(1,128)S(1)} %collective-permute-done.19, f32[18,1,128]{2,1,0:T(1,128)S(1)} %collective-permute-done.18, ...), kind=kLoop, calls=%fused_computation.101 | loop fusion | flops 8650752 | bytes 9717792 | tf_op jit(solution)/shard_map/div | solution.py:35
  148.5 3.9 collective-permute-start.21
  155.2 7.0 %fusion.67 = (f32[16,128,128]{2,1,0:T(8,128)S(1)}, f32[16,128,128]{2,1,0:T(8,128)S(1)}) fusion(f32[]{:T(128)} %bitcast.15, s32[16,128,128]{2,1,0:T(8,128)S(1)} %copy-done, f32[]{:T(128)} %bitcast.14, f32[]{:T(128)} %bitcast.13, f32[]{:T(128)} %bitcast.12, f32[]{:T(128)} %bitcast.11, f32[]{:T(128)} %bitcast.10, f32[]{:T(128)} %bitcast.9, f32[]{:T(128)} %bitcast.8, ...), kind=kLoop, calls=%fused_computation.215 | loop fusion | flops 9437184 | bytes 9586720 | tf_op jit(solution)/shard_map/mul | solution.py:42
  162.2 5.1 %collective-permute-start.5 = (f32[1,128,128]{2,1,0:T(8,128)S(1)}, f32[1,128,128]{2,1,0:T(8,128)S(1)}, u32[]{:S(2)}, u32[]{:S(2)}) collective-permute-start(f32[1,128,128]{2,1,0:T(8,128)S(1)} %get-tuple-element.33), channel_id=1, source_target_pairs={{0,8},{8,16},{16,24},{24,32},{32,40},{40,48},{48,56},{56,64},{64,7... | collective-permute-start | bytes 196616 | tf_op jit(solution)/shard_map/ppermute | solution.py:14
  169.3 4.4 collective-permute-start.23
  175.1 5.8 %collective-permute-start.7 = (f32[18,1,128]{2,1,0:T(1,128)S(1)}, f32[18,1,128]{2,1,0:T(1,128)S(1)}, u32[]{:S(2)}, u32[]{:S(2)}) collective-permute-start(f32[18,1,128]{2,1,0:T(1,128)S(1)} %get-tuple-element.17), channel_id=1, source_target_pairs={{0,1},{1,2},{2,3},{3,4},{4,5},{5,6},{6,7},{8,9},{9,10},{10,11},{11... | collective-permute-start | bytes 27656 | tf_op jit(solution)/shard_map/ppermute | solution.py:14
  183.0 7.1 %fusion.26 = f32[16,128,128]{2,1,0:T(8,128)S(1)} fusion(f32[16,128,128]{2,1,0:T(8,128)S(1)} %bitcast.23, f32[18,130,130]{2,1,0:T(8,128)S(1)} %select_maximum_fusion.8, f32[18,1,128]{2,1,0:T(1,128)S(1)} %collective-permute-done.23, f32[1,128,128]{2,1,0:T(8,128)S(1)} %collective-permute-done.20, f32[16,128,128]{2,1,0:T(8,128)S(1)} %fusion.34, ...), kind=kLoop, calls=%fused_computation.83 | loop fusion | flops 9699328 | bytes 8538144 | tf_op jit(solution)/shard_map/div | solution.py:35
  190.1 5.7 %collective-permute-start.25 = (f32[1,128,128]{2,1,0:T(8,128)S(1)}, f32[1,128,128]{2,1,0:T(8,128)S(1)}, u32[]{:S(2)}, u32[]{:S(2)}) collective-permute-start(f32[1,128,128]{2,1,0:T(8,128)S(1)} %get-tuple-element.39), channel_id=1, source_target_pairs={{0,8},{8,16},{16,24},{24,32},{32,40},{40,48},{48,56},{56,64},{64,7... | collective-permute-start | bytes 196616 | tf_op jit(solution)/shard_map/ppermute | solution.py:14
  198.8 7.1 %fusion.66 = (f32[16,128,128]{2,1,0:T(8,128)S(1)}, f32[16,128,128]{2,1,0:T(8,128)S(1)}) fusion(f32[]{:T(128)} %bitcast.15, s32[16,128,128]{2,1,0:T(8,128)S(1)} %copy-done, f32[]{:T(128)} %bitcast.14, f32[]{:T(128)} %bitcast.13, f32[]{:T(128)} %bitcast.12, f32[]{:T(128)} %bitcast.11, f32[]{:T(128)} %bitcast.10, f32[]{:T(128)} %bitcast.9, f32[]{:T(128)} %bitcast.8, ...), kind=kLoop, calls=%fused_computation.214 | loop fusion | flops 9961472 | bytes 10635296 | tf_op jit(solution)/shard_map/mul | solution.py:42
  206.0 4.6 %collective-permute-start.27 = (f32[18,1,128]{2,1,0:T(1,128)S(1)}, f32[18,1,128]{2,1,0:T(1,128)S(1)}, u32[]{:S(2)}, u32[]{:S(2)}) collective-permute-start(f32[18,1,128]{2,1,0:T(1,128)S(1)} %get-tuple-element.23), channel_id=1, source_target_pairs={{0,1},{1,2},{2,3},{3,4},{4,5},{5,6},{6,7},{8,9},{9,10},{10,11},{11... | collective-permute-start | bytes 27656 | tf_op jit(solution)/shard_map/ppermute | solution.py:14
  211.8 6.0 %collective-permute-start.9 = (f32[1,128,128]{2,1,0:T(8,128)S(1)}, f32[1,128,128]{2,1,0:T(8,128)S(1)}, u32[]{:S(2)}, u32[]{:S(2)}) collective-permute-start(f32[1,128,128]{2,1,0:T(8,128)S(1)} %get-tuple-element.31), channel_id=1, source_target_pairs={{0,8},{8,16},{16,24},{24,32},{32,40},{40,48},{48,56},{56,64},{64,7... | collective-permute-start | bytes 196616 | tf_op jit(solution)/shard_map/ppermute | solution.py:14
  220.6 7.1 %fusion.18 = f32[16,128,128]{2,1,0:T(8,128)S(1)} fusion(f32[16,128,128]{2,1,0:T(8,128)S(1)} %bitcast.25, f32[18,130,130]{2,1,0:T(8,128)S(1)} %select_maximum_fusion.4, f32[18,1,128]{2,1,0:T(1,128)S(1)} %collective-permute-done.27, f32[1,128,128]{2,1,0:T(8,128)S(1)} %collective-permute-done.24, f32[16,128,128]{2,1,0:T(8,128)S(1)} %fusion.26, ...), kind=kLoop, calls=%fused_computation.65 | loop fusion | flops 9699328 | bytes 8538144 | tf_op jit(solution)/shard_map/div | solution.py:35
  227.7 5.1 %collective-permute-start.29 = (f32[1,128,128]{2,1,0:T(8,128)S(1)}, f32[1,128,128]{2,1,0:T(8,128)S(1)}, u32[]{:S(2)}, u32[]{:S(2)}) collective-permute-start(f32[1,128,128]{2,1,0:T(8,128)S(1)} %get-tuple-element.37), channel_id=1, source_target_pairs={{0,8},{8,16},{16,24},{24,32},{32,40},{40,48},{48,56},{56,64},{64,7... | collective-permute-start | bytes 196616 | tf_op jit(solution)/shard_map/ppermute | solution.py:14
  234.9 4.6 %collective-permute-start.11 = (f32[18,1,128]{2,1,0:T(1,128)S(1)}, f32[18,1,128]{2,1,0:T(1,128)S(1)}, u32[]{:S(2)}, u32[]{:S(2)}) collective-permute-start(f32[18,1,128]{2,1,0:T(1,128)S(1)} %get-tuple-element.15), channel_id=1, source_target_pairs={{0,1},{1,2},{2,3},{3,4},{4,5},{5,6},{6,7},{8,9},{9,10},{10,11},{11... | collective-permute-start | bytes 27656 | tf_op jit(solution)/shard_map/ppermute | solution.py:14
  240.8 5.8 %collective-permute-start.31 = (f32[18,1,128]{2,1,0:T(1,128)S(1)}, f32[18,1,128]{2,1,0:T(1,128)S(1)}, u32[]{:S(2)}, u32[]{:S(2)}) collective-permute-start(f32[18,1,128]{2,1,0:T(1,128)S(1)} %get-tuple-element.21), channel_id=1, source_target_pairs={{0,1},{1,2},{2,3},{3,4},{4,5},{5,6},{6,7},{8,9},{9,10},{10,11},{11... | collective-permute-start | bytes 27656 | tf_op jit(solution)/shard_map/ppermute | solution.py:14
  248.7 3.2 collective-permute-done.30
  252.7 10.1 %fusion.10 = (f32[16,128,128]{2,1,0:T(8,128)S(1)}, f32[16,128,128]{2,1,0:T(8,128)S(1)}) fusion(f32[16,128,128]{2,1,0:T(8,128)S(1)} %get-tuple-element.10, f32[16,128,128]{2,1,0:T(8,128)S(1)} %fusion.26, f32[16,128,128]{2,1,0:T(8,128)S(1)} %bitcast.26, f32[18,130,130]{2,1,0:T(8,128)S(1)} %select_maximum_fusion, f32[18,1,128]{2,1,0:T(1,128)S(1)} %collective-permute-done.31, ...), kind=kLoop, calls=%fused_computation.47 | loop fusion | flops 18087936 | bytes 19173408 | tf_op jit(solution)/shard_map/add | solution.py:81
  262.8 5.6 %fusion.65 = f32[16,128,128]{2,1,0:T(8,128)S(1)} fusion(f32[16,128,128]{2,1,0:T(8,128)S(1)} %get-tuple-element.4, f32[]{:T(128)} %bitcast.15, s32[16,128,128]{2,1,0:T(8,128)S(1)} %copy-done, f32[]{:T(128)} %bitcast.14, f32[]{:T(128)} %bitcast.13, f32[]{:T(128)} %bitcast.12, f32[]{:T(128)} %bitcast.11, f32[]{:T(128)} %bitcast.10, f32[]{:T(128)} %bitcast.9, ...), kind=kLoop, calls=%fused_computation.213 | loop fusion | flops 4456448 | bytes 3145760 | tf_op jit(solution)/shard_map/mul | solution.py:42
  269.4 6.9 %collective-permute-start.13 = (f32[1,128,128]{2,1,0:T(8,128)S(1)}, f32[1,128,128]{2,1,0:T(8,128)S(1)}, u32[]{:S(2)}, u32[]{:S(2)}) collective-permute-start(f32[1,128,128]{2,1,0:T(8,128)S(1)} %get-tuple-element.29), channel_id=1, source_target_pairs={{0,8},{8,16},{16,24},{24,32},{32,40},{40,48},{48,56},{56,64},{64,7... | collective-permute-start | bytes 196616 | tf_op jit(solution)/shard_map/ppermute | solution.py:14
  278.2 11.8 %gather_fusion.1 = f32[2048]{0:T(1024)S(1)} fusion(f32[262144]{0:T(1024)S(1)} %bitcast.19, s32[2048]{0:T(1024)S(1)} %broadcast_clamp_fusion), kind=kCustom, calls=%fused_computation.1 | custom fusion | bytes 24576 | tf_op jit(solution)/shard_map/gather | solution.py:82
  290.0 12.9 %scatter_custom_fusion.1 = f32[2048]{0:T(1024)S(1)} fusion(s32[2048]{0:T(1024)S(1)} %bitcast.37, f32[2048]{0:T(1024)S(1)} %multiply_select_fusion, f32[]{:T(128)} %constant.14.clone.1), kind=kCustom, calls=%fused_computation.208 | custom fusion | flops 2048 | bytes 8196 | tf_op jit(solution)/shard_map/scatter-add | solution.py:83
  304.4 3.1 collective-permute-start.15
  308.8 126.4 %reduce-scatter.4.cloned.1.call-done = f32[64,1]{1,0:T(8,128)} async-done(((f32[2048,1]{1,0:T(8,128)}), f32[64,1]{1,0:T(8,128)}) %reduce-scatter.4.cloned.1.call-update) | async-done | bytes 272
  (110 shorter events, 44.8 us)
Async XLA Ops:
  7.2 428.0 %reduce-scatter.4.cloned.1.call-start = ((), (), s32[]{:S(2)}) async-start(), calls=%async_computation.1 | async-start | bytes 1081344
  8.1 122.0 %collective-permute-start.16 = (f32[1,128,128]{2,1,0:T(8,128)S(1)}, f32[1,128,128]{2,1,0:T(8,128)S(1)}, u32[]{:S(2)}, u32[]{:S(2)}) collective-permute-start(f32[1,128,128]{2,1,0:T(8,128)S(1)} %get-tuple-element.45), channel_id=1, source_target_pairs={{8,0},{16,8},{24,16},{32,24},{40,32},{48,40},{56,48},{64,56},{72,6... | collective-permute-start | bytes 196616 | tf_op jit(solution)/shard_map/ppermute | solution.py:17
  13.3 116.7 %collective-permute-start.17 = (f32[1,128,128]{2,1,0:T(8,128)S(1)}, f32[1,128,128]{2,1,0:T(8,128)S(1)}, u32[]{:S(2)}, u32[]{:S(2)}) collective-permute-start(f32[1,128,128]{2,1,0:T(8,128)S(1)} %get-tuple-element.46), channel_id=1, source_target_pairs={{0,8},{8,16},{16,24},{24,32},{32,40},{40,48},{48,56},{56,64},{64,7... | collective-permute-start | bytes 196616 | tf_op jit(solution)/shard_map/ppermute | solution.py:14
  122.4 11.6 %collective-permute-start.1 = (f32[1,128,128]{2,1,0:T(8,128)S(1)}, f32[1,128,128]{2,1,0:T(8,128)S(1)}, u32[]{:S(2)}, u32[]{:S(2)}) collective-permute-start(f32[1,128,128]{2,1,0:T(8,128)S(1)} %get-tuple-element.35), channel_id=1, source_target_pairs={{0,8},{8,16},{16,24},{24,32},{32,40},{40,48},{48,56},{56,64},{64,7... | collective-permute-start | bytes 196616 | tf_op jit(solution)/shard_map/ppermute | solution.py:14
  126.0 8.1 %collective-permute-start = (f32[1,128,128]{2,1,0:T(8,128)S(1)}, f32[1,128,128]{2,1,0:T(8,128)S(1)}, u32[]{:S(2)}, u32[]{:S(2)}) collective-permute-start(f32[1,128,128]{2,1,0:T(8,128)S(1)} %get-tuple-element.36), channel_id=1, source_target_pairs={{8,0},{16,8},{24,16},{32,24},{40,32},{48,40},{56,48},{64,56},{72,6... | collective-permute-start | bytes 196616 | tf_op jit(solution)/shard_map/ppermute | solution.py:17
  130.2 10.1 %collective-permute-start.19 = (f32[18,1,128]{2,1,0:T(1,128)S(1)}, f32[18,1,128]{2,1,0:T(1,128)S(1)}, u32[]{:S(2)}, u32[]{:S(2)}) collective-permute-start(f32[18,1,128]{2,1,0:T(1,128)S(1)} %get-tuple-element.27), channel_id=1, source_target_pairs={{0,1},{1,2},{2,3},{3,4},{4,5},{5,6},{6,7},{8,9},{9,10},{10,11},{11... | collective-permute-start | bytes 27656 | tf_op jit(solution)/shard_map/ppermute | solution.py:14
  132.7 7.6 %collective-permute-start.18 = (f32[18,1,128]{2,1,0:T(1,128)S(1)}, f32[18,1,128]{2,1,0:T(1,128)S(1)}, u32[]{:S(2)}, u32[]{:S(2)}) collective-permute-start(f32[18,1,128]{2,1,0:T(1,128)S(1)} %get-tuple-element.28), channel_id=1, source_target_pairs={{1,0},{2,1},{3,2},{4,3},{5,4},{6,5},{7,6},{9,8},{10,9},{11,10},{12... | collective-permute-start | bytes 27656 | tf_op jit(solution)/shard_map/ppermute | solution.py:17
  134.1 20.3 %collective-permute-start.3 = (f32[18,1,128]{2,1,0:T(1,128)S(1)}, f32[18,1,128]{2,1,0:T(1,128)S(1)}, u32[]{:S(2)}, u32[]{:S(2)}) collective-permute-start(f32[18,1,128]{2,1,0:T(1,128)S(1)} %get-tuple-element.19), channel_id=1, source_target_pairs={{0,1},{1,2},{2,3},{3,4},{4,5},{5,6},{6,7},{8,9},{9,10},{10,11},{11... | collective-permute-start | bytes 27656 | tf_op jit(solution)/shard_map/ppermute | solution.py:14
  139.0 15.4 %collective-permute-start.2 = (f32[18,1,128]{2,1,0:T(1,128)S(1)}, f32[18,1,128]{2,1,0:T(1,128)S(1)}, u32[]{:S(2)}, u32[]{:S(2)}) collective-permute-start(f32[18,1,128]{2,1,0:T(1,128)S(1)} %get-tuple-element.20), channel_id=1, source_target_pairs={{1,0},{2,1},{3,2},{4,3},{5,4},{6,5},{7,6},{9,8},{10,9},{11,10},{12... | collective-permute-start | bytes 27656 | tf_op jit(solution)/shard_map/ppermute | solution.py:17
  148.5 20.8 %collective-permute-start.21 = (f32[1,128,128]{2,1,0:T(8,128)S(1)}, f32[1,128,128]{2,1,0:T(8,128)S(1)}, u32[]{:S(2)}, u32[]{:S(2)}) collective-permute-start(f32[1,128,128]{2,1,0:T(8,128)S(1)} %get-tuple-element.41), channel_id=1, source_target_pairs={{0,8},{8,16},{16,24},{24,32},{32,40},{40,48},{48,56},{56,64},{64,7... | collective-permute-start | bytes 196616 | tf_op jit(solution)/shard_map/ppermute | solution.py:14
  152.4 16.9 %collective-permute-start.20 = (f32[1,128,128]{2,1,0:T(8,128)S(1)}, f32[1,128,128]{2,1,0:T(8,128)S(1)}, u32[]{:S(2)}, u32[]{:S(2)}) collective-permute-start(f32[1,128,128]{2,1,0:T(8,128)S(1)} %get-tuple-element.42), channel_id=1, source_target_pairs={{8,0},{16,8},{24,16},{32,24},{40,32},{48,40},{56,48},{64,56},{72,6... | collective-permute-start | bytes 196616 | tf_op jit(solution)/shard_map/ppermute | solution.py:17
  162.2 12.9 %collective-permute-start.5 = (f32[1,128,128]{2,1,0:T(8,128)S(1)}, f32[1,128,128]{2,1,0:T(8,128)S(1)}, u32[]{:S(2)}, u32[]{:S(2)}) collective-permute-start(f32[1,128,128]{2,1,0:T(8,128)S(1)} %get-tuple-element.33), channel_id=1, source_target_pairs={{0,8},{8,16},{16,24},{24,32},{32,40},{40,48},{48,56},{56,64},{64,7... | collective-permute-start | bytes 196616 | tf_op jit(solution)/shard_map/ppermute | solution.py:14
  167.4 7.7 %collective-permute-start.4 = (f32[1,128,128]{2,1,0:T(8,128)S(1)}, f32[1,128,128]{2,1,0:T(8,128)S(1)}, u32[]{:S(2)}, u32[]{:S(2)}) collective-permute-start(f32[1,128,128]{2,1,0:T(8,128)S(1)} %get-tuple-element.34), channel_id=1, source_target_pairs={{8,0},{16,8},{24,16},{32,24},{40,32},{48,40},{56,48},{64,56},{72,6... | collective-permute-start | bytes 196616 | tf_op jit(solution)/shard_map/ppermute | solution.py:17
  169.3 12.9 %collective-permute-start.23 = (f32[18,1,128]{2,1,0:T(1,128)S(1)}, f32[18,1,128]{2,1,0:T(1,128)S(1)}, u32[]{:S(2)}, u32[]{:S(2)}) collective-permute-start(f32[18,1,128]{2,1,0:T(1,128)S(1)} %get-tuple-element.25), channel_id=1, source_target_pairs={{0,1},{1,2},{2,3},{3,4},{4,5},{5,6},{6,7},{8,9},{9,10},{10,11},{11... | collective-permute-start | bytes 27656 | tf_op jit(solution)/shard_map/ppermute | solution.py:14
  173.8 8.4 %collective-permute-start.22 = (f32[18,1,128]{2,1,0:T(1,128)S(1)}, f32[18,1,128]{2,1,0:T(1,128)S(1)}, u32[]{:S(2)}, u32[]{:S(2)}) collective-permute-start(f32[18,1,128]{2,1,0:T(1,128)S(1)} %get-tuple-element.26), channel_id=1, source_target_pairs={{1,0},{2,1},{3,2},{4,3},{5,4},{6,5},{7,6},{9,8},{10,9},{11,10},{12... | collective-permute-start | bytes 27656 | tf_op jit(solution)/shard_map/ppermute | solution.py:17
  175.1 22.8 %collective-permute-start.7 = (f32[18,1,128]{2,1,0:T(1,128)S(1)}, f32[18,1,128]{2,1,0:T(1,128)S(1)}, u32[]{:S(2)}, u32[]{:S(2)}) collective-permute-start(f32[18,1,128]{2,1,0:T(1,128)S(1)} %get-tuple-element.17), channel_id=1, source_target_pairs={{0,1},{1,2},{2,3},{3,4},{4,5},{5,6},{6,7},{8,9},{9,10},{10,11},{11... | collective-permute-start | bytes 27656 | tf_op jit(solution)/shard_map/ppermute | solution.py:14
  180.9 17.1 %collective-permute-start.6 = (f32[18,1,128]{2,1,0:T(1,128)S(1)}, f32[18,1,128]{2,1,0:T(1,128)S(1)}, u32[]{:S(2)}, u32[]{:S(2)}) collective-permute-start(f32[18,1,128]{2,1,0:T(1,128)S(1)} %get-tuple-element.18), channel_id=1, source_target_pairs={{1,0},{2,1},{3,2},{4,3},{5,4},{6,5},{7,6},{9,8},{10,9},{11,10},{12... | collective-permute-start | bytes 27656 | tf_op jit(solution)/shard_map/ppermute | solution.py:17
  190.1 15.8 %collective-permute-start.25 = (f32[1,128,128]{2,1,0:T(8,128)S(1)}, f32[1,128,128]{2,1,0:T(8,128)S(1)}, u32[]{:S(2)}, u32[]{:S(2)}) collective-permute-start(f32[1,128,128]{2,1,0:T(8,128)S(1)} %get-tuple-element.39), channel_id=1, source_target_pairs={{0,8},{8,16},{16,24},{24,32},{32,40},{40,48},{48,56},{56,64},{64,7... | collective-permute-start | bytes 196616 | tf_op jit(solution)/shard_map/ppermute | solution.py:14
  195.8 10.1 %collective-permute-start.24 = (f32[1,128,128]{2,1,0:T(8,128)S(1)}, f32[1,128,128]{2,1,0:T(8,128)S(1)}, u32[]{:S(2)}, u32[]{:S(2)}) collective-permute-start(f32[1,128,128]{2,1,0:T(8,128)S(1)} %get-tuple-element.40), channel_id=1, source_target_pairs={{8,0},{16,8},{24,16},{32,24},{40,32},{48,40},{56,48},{64,56},{72,6... | collective-permute-start | bytes 196616 | tf_op jit(solution)/shard_map/ppermute | solution.py:17
  206.0 13.9 %collective-permute-start.27 = (f32[18,1,128]{2,1,0:T(1,128)S(1)}, f32[18,1,128]{2,1,0:T(1,128)S(1)}, u32[]{:S(2)}, u32[]{:S(2)}) collective-permute-start(f32[18,1,128]{2,1,0:T(1,128)S(1)} %get-tuple-element.23), channel_id=1, source_target_pairs={{0,1},{1,2},{2,3},{3,4},{4,5},{5,6},{6,7},{8,9},{9,10},{10,11},{11... | collective-permute-start | bytes 27656 | tf_op jit(solution)/shard_map/ppermute | solution.py:14
  210.5 9.3 %collective-permute-start.26 = (f32[18,1,128]{2,1,0:T(1,128)S(1)}, f32[18,1,128]{2,1,0:T(1,128)S(1)}, u32[]{:S(2)}, u32[]{:S(2)}) collective-permute-start(f32[18,1,128]{2,1,0:T(1,128)S(1)} %get-tuple-element.24), channel_id=1, source_target_pairs={{1,0},{2,1},{3,2},{4,3},{5,4},{6,5},{7,6},{9,8},{10,9},{11,10},{12... | collective-permute-start | bytes 27656 | tf_op jit(solution)/shard_map/ppermute | solution.py:17
  211.8 23.0 %collective-permute-start.9 = (f32[1,128,128]{2,1,0:T(8,128)S(1)}, f32[1,128,128]{2,1,0:T(8,128)S(1)}, u32[]{:S(2)}, u32[]{:S(2)}) collective-permute-start(f32[1,128,128]{2,1,0:T(8,128)S(1)} %get-tuple-element.31), channel_id=1, source_target_pairs={{0,8},{8,16},{16,24},{24,32},{32,40},{40,48},{48,56},{56,64},{64,7... | collective-permute-start | bytes 196616 | tf_op jit(solution)/shard_map/ppermute | solution.py:14
  217.9 16.9 %collective-permute-start.8 = (f32[1,128,128]{2,1,0:T(8,128)S(1)}, f32[1,128,128]{2,1,0:T(8,128)S(1)}, u32[]{:S(2)}, u32[]{:S(2)}) collective-permute-start(f32[1,128,128]{2,1,0:T(8,128)S(1)} %get-tuple-element.32), channel_id=1, source_target_pairs={{8,0},{16,8},{24,16},{32,24},{40,32},{48,40},{56,48},{64,56},{72,6... | collective-permute-start | bytes 196616 | tf_op jit(solution)/shard_map/ppermute | solution.py:17
  227.7 13.0 %collective-permute-start.29 = (f32[1,128,128]{2,1,0:T(8,128)S(1)}, f32[1,128,128]{2,1,0:T(8,128)S(1)}, u32[]{:S(2)}, u32[]{:S(2)}) collective-permute-start(f32[1,128,128]{2,1,0:T(8,128)S(1)} %get-tuple-element.37), channel_id=1, source_target_pairs={{0,8},{8,16},{16,24},{24,32},{32,40},{40,48},{48,56},{56,64},{64,7... | collective-permute-start | bytes 196616 | tf_op jit(solution)/shard_map/ppermute | solution.py:14
  232.9 7.9 %collective-permute-start.28 = (f32[1,128,128]{2,1,0:T(8,128)S(1)}, f32[1,128,128]{2,1,0:T(8,128)S(1)}, u32[]{:S(2)}, u32[]{:S(2)}) collective-permute-start(f32[1,128,128]{2,1,0:T(8,128)S(1)} %get-tuple-element.38), channel_id=1, source_target_pairs={{8,0},{16,8},{24,16},{32,24},{40,32},{48,40},{56,48},{64,56},{72,6... | collective-permute-start | bytes 196616 | tf_op jit(solution)/shard_map/ppermute | solution.py:17
  234.9 13.0 %collective-permute-start.11 = (f32[18,1,128]{2,1,0:T(1,128)S(1)}, f32[18,1,128]{2,1,0:T(1,128)S(1)}, u32[]{:S(2)}, u32[]{:S(2)}) collective-permute-start(f32[18,1,128]{2,1,0:T(1,128)S(1)} %get-tuple-element.15), channel_id=1, source_target_pairs={{0,1},{1,2},{2,3},{3,4},{4,5},{5,6},{6,7},{8,9},{9,10},{10,11},{11... | collective-permute-start | bytes 27656 | tf_op jit(solution)/shard_map/ppermute | solution.py:14
  239.4 8.4 %collective-permute-start.10 = (f32[18,1,128]{2,1,0:T(1,128)S(1)}, f32[18,1,128]{2,1,0:T(1,128)S(1)}, u32[]{:S(2)}, u32[]{:S(2)}) collective-permute-start(f32[18,1,128]{2,1,0:T(1,128)S(1)} %get-tuple-element.16), channel_id=1, source_target_pairs={{1,0},{2,1},{3,2},{4,3},{5,4},{6,5},{7,6},{9,8},{10,9},{11,10},{12... | collective-permute-start | bytes 27656 | tf_op jit(solution)/shard_map/ppermute | solution.py:17
  240.8 7.9 %collective-permute-start.31 = (f32[18,1,128]{2,1,0:T(1,128)S(1)}, f32[18,1,128]{2,1,0:T(1,128)S(1)}, u32[]{:S(2)}, u32[]{:S(2)}) collective-permute-start(f32[18,1,128]{2,1,0:T(1,128)S(1)} %get-tuple-element.21), channel_id=1, source_target_pairs={{0,1},{1,2},{2,3},{3,4},{4,5},{5,6},{6,7},{8,9},{9,10},{10,11},{11... | collective-permute-start | bytes 27656 | tf_op jit(solution)/shard_map/ppermute | solution.py:14
  269.4 35.0 %collective-permute-start.13 = (f32[1,128,128]{2,1,0:T(8,128)S(1)}, f32[1,128,128]{2,1,0:T(8,128)S(1)}, u32[]{:S(2)}, u32[]{:S(2)}) collective-permute-start(f32[1,128,128]{2,1,0:T(8,128)S(1)} %get-tuple-element.29), channel_id=1, source_target_pairs={{0,8},{8,16},{16,24},{24,32},{32,40},{40,48},{48,56},{56,64},{64,7... | collective-permute-start | bytes 196616 | tf_op jit(solution)/shard_map/ppermute | solution.py:14
  276.3 28.1 %collective-permute-start.12 = (f32[1,128,128]{2,1,0:T(8,128)S(1)}, f32[1,128,128]{2,1,0:T(8,128)S(1)}, u32[]{:S(2)}, u32[]{:S(2)}) collective-permute-start(f32[1,128,128]{2,1,0:T(8,128)S(1)} %get-tuple-element.30), channel_id=1, source_target_pairs={{8,0},{16,8},{24,16},{32,24},{40,32},{48,40},{56,48},{64,56},{72,6... | collective-permute-start | bytes 196616 | tf_op jit(solution)/shard_map/ppermute | solution.py:17
  304.4 132.1 %collective-permute-start.15 = (f32[18,1,128]{2,1,0:T(1,128)S(1)}, f32[18,1,128]{2,1,0:T(1,128)S(1)}, u32[]{:S(2)}, u32[]{:S(2)}) collective-permute-start(f32[18,1,128]{2,1,0:T(1,128)S(1)} %get-tuple-element.13), channel_id=1, source_target_pairs={{0,1},{1,2},{2,3},{3,4},{4,5},{5,6},{6,7},{8,9},{9,10},{10,11},{11... | collective-permute-start | bytes 27656 | tf_op jit(solution)/shard_map/ppermute | solution.py:14
  307.5 129.0 %collective-permute-start.14 = (f32[18,1,128]{2,1,0:T(1,128)S(1)}, f32[18,1,128]{2,1,0:T(1,128)S(1)}, u32[]{:S(2)}, u32[]{:S(2)}) collective-permute-start(f32[18,1,128]{2,1,0:T(1,128)S(1)} %get-tuple-element.14), channel_id=1, source_target_pairs={{1,0},{2,1},{3,2},{4,3},{5,4},{6,5},{7,6},{9,8},{10,9},{11,10},{12... | collective-permute-start | bytes 27656 | tf_op jit(solution)/shard_map/ppermute | solution.py:17
  (11 other events, 255.1 us)
Sparse Core Ops, SparseCore 0:
  304.5 130.6 reduce-scatter.3
where the time goes:
time: 453 us; the launch traced here: 447 us
  waiting for transfers between devices  130 us (29%)
  starting transfers between devices  106 us (23%)
  other arithmetic  96.8 us (21%)
  blocking collectives  66.3 us (15%)
  local copies, waits for them, and re-layouts  32.4 us (7%)
  between operations  15.7 us (3%)
    unnamed x2, waiting for transfers between devices  126 us
    ppermute x16, starting transfers between devices, extended(): lax.ppermute(lax.slice_in_dim(block, block.shape[dim] - width, None, axis...  74.9 us
    squeeze x1, blocking collectives, local(): slot_gamma = jnp.where(live, 0.25 * strip[0][safe_patch], jnp.float32(0.0))  66.3 us
    ppermute x16, starting transfers between devices, extended(): lax.ppermute(lax.slice_in_dim(block, 0, width, axis=dim), axis, backward)  31.2 us
    mul x4, other arithmetic, sweep(): m_new = m_low + 2.0 * weight + apply_laplace(c2 * weight)  26.7 us
    div x3, other arithmetic, sweep(): states.append((drive - (1.0 - gamma) * prev) / (1.0 + gamma))  21.5 us
    scatter-add x1, other arithmetic, local(): jnp.zeros((c2.size,), jnp.float32).at[safe_cell].add(slot_gamma)  14.4 us
    scatter-add x1, other arithmetic, local(): jnp.zeros((strip.shape[1],), jnp.float32).at[safe_patch].add(values)  12.9 us
  transfers between devices with their start and end apart: 33, of which 2 were waited for; matrix products, arithmetic and copies ran while one was open for 24% of the time, Pallas kernels for 0%

commit v1 on v0

v1 whole, which is shorter than its diff:
```python
import jax
import jax.numpy as jnp
from jax import lax
from jax.experimental import pallas as pl
from jax.experimental.pallas import tpu as pltpu
from jax.sharding import PartitionSpec as P

MESH = pl.DeviceIdType.MESH
F32 = jnp.float32
BF16 = jnp.bfloat16
CX, CY, NZ = 16, 128, 128
SLOTS = 2048
ROWS = 32
COLS = 8
SHARE = 64
PX, PY = CX + 2, CY + 16


def natural(step):
    return pl.ds(step, 8, 16)


def lane_masks():
    lane = lax.broadcasted_iota(jnp.int32, (8, NZ), 1)
    return lane == 0, lane == NZ - 1


def around(field, x, row, masks):
    here = field[x, pl.ds(row, 8), :]
    total = field[x - 1, pl.ds(row, 8), :] + field[x + 1, pl.ds(row, 8), :]
    total = total + (field[x, pl.ds(row - 8, 8), :] + field[x, pl.ds(row + 8, 8), :])
    low = jnp.where(masks[0], 0.0, pltpu.roll(here, 1, 1))
    high = jnp.where(masks[1], 0.0, pltpu.roll(here, NZ - 1, 1))
    return here, total + (low + high) - 6.0 * here


def fill_sides(field, x):
    field[x, 1:8, :] = field[x, CY : CY + 7, :]
    field[x, CY + 8 : CY + 15, :] = field[x, 9:16, :]


def kernel(
    p0_in, p1_in, m4_in, m5_in, mat_in, speed, adm, cell, patch,
    g0_out, g1_out, pg_out,
    raw, kinds, fields, c2, q, before, base, diff, weights, last, result,
    side, rt, bt, vt, gt, gsum, own, table, parts, arrived,
    load_sem, store_sem, send_sem, recv_sem, share_sem,
):
    row = lax.axis_index("row")
    col = lax.axis_index("col")
    masks = lane_masks()

    names = (p1_in, mat_in, p0_in, m5_in, m4_in)
    loads = [
        pltpu.make_async_copy(ref, kinds if n == 1 else raw.at[n], load_sem.at[n])
        for n, ref in enumerate(names)
    ]
    for load in loads:
        load.start()

    barrier = pltpu.get_barrier_semaphore()

    def greet(step, carry):
        pl.semaphore_signal(
            barrier, inc=1, device_id=(lax.rem(row + step, ROWS), col), device_id_type=MESH
        )
        return carry

    lax.fori_loop(1, ROWS, greet, 0)
    for step in (1, COLS - 1):
        pl.semaphore_signal(
            barrier, inc=1, device_id=(row, lax.rem(col + step, COLS)), device_id_type=MESH
        )

    zero_plane = jnp.zeros((CY, NZ), F32)
    zero_row = jnp.zeros((CX, 1, NZ), F32)

    @pl.when(row == 0)
    def _():
        for f in range(8):
            fields[f, 0, 8 : 8 + CY, :] = zero_plane

    @pl.when(row == ROWS - 1)
    def _():
        for f in range(8):
            fields[f, PX - 1, 8 : 8 + CY, :] = zero_plane

    @pl.when(col == 0)
    def _():
        for f in range(8):
            fields[f, 1 : 1 + CX, 0:1, :] = zero_row

    @pl.when(col == COLS - 1)
    def _():
        for f in range(8):
            fields[f, 1 : 1 + CX, PY - 1 : PY, :] = zero_row

    own[...] = jnp.zeros_like(own)
    own[0, :, 0:SHARE] = adm[...]
    table[pl.ds(row, 1)] = own[...]

    pl.semaphore_wait(barrier, ROWS + 1)

    sides = (
        (row < ROWS - 1, (row + 1, col)),
        (row > 0, (row - 1, col)),
        (col < COLS - 1, (row, col + 1)),
        (col > 0, (row, col - 1)),
    )
    comes = (row > 0, row < ROWS - 1, col > 0, col < COLS - 1)

    def copies(f):
        field = fields.at[f]
        pairs = (
            (field.at[CX, 8 : 8 + CY, :], field.at[0, 8 : 8 + CY, :]),
            (field.at[1, 8 : 8 + CY, :], field.at[PX - 1, 8 : 8 + CY, :]),
            (field.at[1 : 1 + CX, CY + 7 : CY + 8, :], field.at[1 : 1 + CX, 0:1, :]),
            (field.at[1 : 1 + CX, 8:9, :], field.at[1 : 1 + CX, PY - 1 : PY, :]),
        )
        if f == 0:
            pairs = (
                (p1_in.at[CX - 1], side.at[0]),
                (p1_in.at[0], side.at[1]),
                (p1_in.at[:, CY - 1 : CY, :], pairs[2][1]),
                (p1_in.at[:, 0:1, :], pairs[3][1]),
            )
        return [
            pltpu.make_async_remote_copy(
                src, dst, send_sem.at[f, d], recv_sem.at[f, d],
                device_id=sides[d][1], device_id_type=MESH,
            )
            for d, (src, dst) in enumerate(pairs)
        ]

    def send(f):
        for d, copy in enumerate(copies(f)):
            pl.when(sides[d][0])(copy.start)

    def receive(f):
        for d, copy in enumerate(copies(f)):
            pl.when(comes[d])(copy.wait_recv)

    def sent(f):
        for d, copy in enumerate(copies(f)):
            pl.when(sides[d][0])(copy.wait_send)

    send(0)

    def share(source, sem):
        def start(step, carry):
            to = lax.rem(row + step, ROWS)
            pltpu.make_async_remote_copy(
                source(to), (table if sem == 0 else arrived).at[pl.ds(row, 1)],
                share_sem.at[2 * sem], share_sem.at[2 * sem + 1],
                device_id=(to, col), device_id_type=MESH,
            ).start()
            return carry

        lax.fori_loop(1, ROWS, start, 0)

    def shared(buffer, which):
        rest = buffer.at[pl.ds(0, ROWS - 1)]
        pltpu.make_async_copy(rest, rest, share_sem.at[which]).wait()

    share(lambda to: own, 0)

    cells = cell[...]
    spots = patch[...]
    depth = cells & (NZ - 1)
    y = (cells >> 7) & (CY - 1)
    line = (cells >> 14) * CY + (y & 15) * 8 + (y >> 4)
    owner = spots >> 6
    place = spots & (SHARE - 1)

    def build(block, carry):
        start = pl.multiple_of(block * 16, 16)
        index = lax.broadcasted_iota(jnp.int32, (16, SLOTS), 0) + start
        rt[pl.ds(start, 16), :] = jnp.where(index == line, 1.0, 0.0).astype(BF16)
        return carry

    lax.fori_loop(0, SLOTS // 16, build, 0)
    index = lax.broadcasted_iota(jnp.int32, (NZ, SLOTS), 0)
    bt[...] = jnp.where(index == place, 1.0, 0.0).astype(BF16)

    loads[0].wait()
    loads[1].wait()
    speeds = [speed[n] for n in range(8)]

    def arrange(x, carry):
        for t in range(16):
            fields[0, x + 1, pl.ds(8 + 8 * t, 8), :] = raw[0, x, natural(t), :]
            kind = kinds[x, natural(t), :]
            value = jnp.full((8, NZ), speeds[0], F32)
            for n in range(1, 8):
                value = jnp.where(kind == n, speeds[n], value)
            c2[x, pl.ds(8 * t, 8), :] = value
        fill_sides(fields.at[0], x + 1)
        return carry

    lax.fori_loop(0, CX, arrange, 0)

    loads[2].wait()
    loads[3].wait()
    loads[4].wait()

    def arrange_rest(x, carry):
        for t in range(16):
            before[x, pl.ds(8 * t, 8), :] = raw[2, x, natural(t), :]
        return carry

    lax.fori_loop(0, CX, arrange_rest, 0)

    shared(table, 1)
    shared(table, 0)
    strip = 0.25 * table[:, 0, :]
    strip_high = strip.astype(BF16)
    strip_low = (strip - strip_high.astype(F32)).astype(BF16)
    found = jnp.dot(
        jnp.concatenate([strip_high, strip_low], axis=0), bt[...], preferred_element_type=F32
    )
    found = found[:ROWS] + found[ROWS:]
    index = lax.broadcasted_iota(jnp.int32, (ROWS, SLOTS), 0)
    slot = jnp.sum(jnp.where(index == owner, found, 0.0), axis=0, keepdims=True)
    slot_high = slot.astype(BF16).astype(F32)
    slot_low = slot - slot_high
    index = lax.broadcasted_iota(jnp.int32, (NZ, SLOTS), 0)
    vt[0:NZ, :] = jnp.where(index == depth, slot_high, 0.0).astype(BF16)
    vt[NZ : 2 * NZ, :] = jnp.where(index == depth, slot_low, 0.0).astype(BF16)

    def spread(pair, carry):
        start = pl.multiple_of(pair * 256, 256)
        both = lax.dot_general(
            rt[pl.ds(start, 256), :], vt[...], (((1,), (1,)), ((), ())), preferred_element_type=F32
        )
        for half in range(2):
            x = 2 * pair + half
            for t in range(16):
                at = half * CY + 8 * t
                gamma = both[at : at + 8, 0:NZ] + both[at : at + 8, NZ : 2 * NZ]
                here = pl.ds(8 * t, 8)
                scale = 1.0 / (1.0 + gamma)
                q[x, here, :] = scale
                high = raw[3, x, natural(t), :]
                weight = scale * high
                weights[0, x, here, :] = weight
                fields[4, x + 1, pl.ds(8 + 8 * t, 8), :] = c2[x, here, :] * weight
                base[x, here, :] = raw[4, x, natural(t), :] + 2.0 * weight
                diff[x, here, :] = high - 2.0 * weight
            fill_sides(fields.at[4], x + 1)
        return carry

    lax.fori_loop(0, CX // 2, spread, 0)
    send(4)

    def forward(k):
        now = fields.at[k - 1]

        def tile(x, t):
            at = pl.ds(8 * t, 8)
            here, change = around(now, x, 8 + 8 * t, masks)
            old = before[x - 1, at, :] if k == 1 else fields[k - 2, x, pl.ds(8 + 8 * t, 8), :]
            new = old + q[x - 1, at, :] * (2.0 * (here - old) + c2[x - 1, at, :] * change)
            if k == 4:
                last[x - 1, at, :] = new
            else:
                fields[k, x, pl.ds(8 + 8 * t, 8), :] = new

        def done(x):
            if k < 4:
                fill_sides(fields.at[k], x)

        return tile, done

    def adjoint(k):
        f = 8 - k
        now = fields.at[f]

        def tile(x, t):
            at = pl.ds(8 * t, 8)
            here, change = around(now, x, 8 + 8 * t, masks)
            high = base[x - 1, at, :] + change
            if k == 1:
                result[1, x - 1, natural(t), :] = high
                return
            weight = q[x - 1, at, :] * high
            weights[f - 3, x - 1, at, :] = weight
            fields[f + 1, x, pl.ds(8 + 8 * t, 8), :] = c2[x - 1, at, :] * weight
            twice = 2.0 * weight
            base[x - 1, at, :] = diff[x - 1, at, :] + twice
            if k == 2:
                result[0, x - 1, natural(t), :] = high - twice
            else:
                diff[x - 1, at, :] = high - twice

        def done(x):
            if k > 1:
                fill_sides(fields.at[f + 1], x)

        return tile, done

    def inside(step):
        def body(x, carry):
            for t in range(1, 15):
                step[0](x, t)
            return carry

        lax.fori_loop(2, CX, body, 0)

    def outside(step):
        def ends(n, carry):
            x = 1 + n * (CX - 1)
            for t in range(16):
                step[0](x, t)
            step[1](x)
            return carry

        def edges(x, carry):
            for t in (0, 15):
                step[0](x, t)
            step[1](x)
            return carry

        lax.fori_loop(0, 2, ends, 0)
        lax.fori_loop(2, CX, edges, 0)

    inside(forward(1))
    receive(0)
    for n, plane, there in ((0, 0, comes[0]), (1, PX - 1, comes[1])):
        def place_side(n=n, plane=plane):
            for t in range(16):
                fields[0, plane, pl.ds(8 + 8 * t, 8), :] = side[n, natural(t), :]

        pl.when(there)(place_side)
    outside(forward(1))
    send(1)

    for k in (2, 3, 4):
        level = 6 - k
        step = adjoint(level)
        inside(step)
        receive(8 - level)
        outside(step)
        send(9 - level)
        step = forward(k)
        inside(step)
        receive(k - 1)
        outside(step)
        if k < 4:
            send(k)

    first_store = pltpu.make_async_copy(result.at[0], g0_out, store_sem.at[0])
    first_store.start()

    def collect(x, carry):
        for t in range(16):
            at = pl.ds(8 * t, 8)
            inner = pl.ds(8 + 8 * t, 8)
            total = weights[3, x, at, :] * (before[x, at, :] - fields[1, x + 1, inner, :])
            for k in (2, 3):
                total = total + weights[4 - k, x, at, :] * (
                    fields[k - 2, x + 1, inner, :] - fields[k, x + 1, inner, :]
                )
            total = total + weights[0, x, at, :] * (
                fields[2, x + 1, inner, :] - last[x, at, :]
            )
            gsum[at, :] = 0.25 * total
        turned = gsum[...].T
        high = turned.astype(BF16)
        lane = pl.ds(pl.multiple_of(x * CY, CY), CY)
        gt[0:NZ, lane] = high
        gt[NZ : 2 * NZ, lane] = (turned - high.astype(F32)).astype(BF16)
        return carry

    lax.fori_loop(0, CX, collect, 0)
    total = jnp.zeros((2 * ROWS, NZ), F32)
    for chunk in range(SLOTS // 256):
        lanes = slice(256 * chunk, 256 * chunk + 256)
        picked = jnp.dot(gt[...], rt[:, lanes], preferred_element_type=F32)
        picked = picked[:NZ] + picked[NZ:]
        index = lax.broadcasted_iota(jnp.int32, (NZ, 256), 0)
        value = jnp.sum(
            jnp.where(index == depth[:, lanes], picked, 0.0), axis=0, keepdims=True
        )
        high = value.astype(BF16).astype(F32)
        low = value - high
        index = lax.broadcasted_iota(jnp.int32, (ROWS, 256), 0)
        mine = index == owner[:, lanes]
        both = jnp.concatenate(
            [jnp.where(mine, high, 0.0), jnp.where(mine, low, 0.0)], axis=0
        ).astype(BF16)
        total = total + lax.dot_general(
            both, bt[:, lanes], (((1,), (1,)), ((), ())), preferred_element_type=F32
        )
    parts[:, 0, :] = total[:ROWS] + total[ROWS:]
    arrived[pl.ds(row, 1)] = parts[pl.ds(row, 1)]
    share(lambda to: parts.at[pl.ds(to, 1)], 1)

    step = adjoint(1)
    inside(step)
    receive(7)
    outside(step)
    second_store = pltpu.make_async_copy(result.at[1], g1_out, store_sem.at[1])
    second_store.start()

    shared(arrived, 3)
    shared(arrived, 2)
    pg_out[...] = jnp.sum(arrived[...], axis=0)[:, 0:SHARE]
    for f in range(8):
        sent(f)
    first_store.wait()
    second_store.wait()


def local(p0, p1, m4, m5, material, speed_sq, admittance, bound_cell, bound_patch):
    block = (CX, CY, NZ)
    anywhere = pl.BlockSpec(memory_space=pl.ANY)
    vmem = pl.BlockSpec(memory_space=pltpu.VMEM)
    return pl.pallas_call(
        kernel,
        out_shape=(
            jax.ShapeDtypeStruct(block, F32),
            jax.ShapeDtypeStruct(block, F32),
            jax.ShapeDtypeStruct((1, SHARE), F32),
        ),
        in_specs=[anywhere] * 5 + [pl.BlockSpec(memory_space=pltpu.SMEM)] + [vmem] * 3,
        out_specs=(anywhere, anywhere, vmem),
        scratch_shapes=[
            pltpu.VMEM((5,) + block, F32),
            pltpu.VMEM(block, jnp.int32),
            pltpu.VMEM((8, PX, PY, NZ), F32),
            pltpu.VMEM(block, F32),
            pltpu.VMEM(block, F32),
            pltpu.VMEM(block, F32),
            pltpu.VMEM(block, F32),
            pltpu.VMEM(block, F32),
            pltpu.VMEM((4,) + block, F32),
            pltpu.VMEM(block, F32),
            pltpu.VMEM((2,) + block, F32),
            pltpu.VMEM((2, CY, NZ), F32),
            pltpu.VMEM((SLOTS, SLOTS), BF16),
            pltpu.VMEM((NZ, SLOTS), BF16),
            pltpu.VMEM((2 * NZ, SLOTS), BF16),
            pltpu.VMEM((2 * NZ, SLOTS), BF16),
            pltpu.VMEM((CY, NZ), F32),
            pltpu.VMEM((1, 1, NZ), F32),
            pltpu.VMEM((ROWS, 1, NZ), F32),
            pltpu.VMEM((ROWS, 1, NZ), F32),
            pltpu.VMEM((ROWS, 1, NZ), F32),
            pltpu.SemaphoreType.DMA((5,)),
            pltpu.SemaphoreType.DMA((2,)),
            pltpu.SemaphoreType.DMA((8, 4)),
            pltpu.SemaphoreType.DMA((8, 4)),
            pltpu.SemaphoreType.DMA((4,)),
        ],
        compiler_params=pltpu.CompilerParams(
            collective_id=0, has_side_effects=True, vmem_limit_bytes=60 << 20
        ),
    )(p0, p1, m4, m5, material, speed_sq, admittance, bound_cell, bound_patch)


def solution(mesh):
    field = P("row", "col", None)
    return jax.shard_map(
        local,
        mesh=mesh,
        in_specs=(field,) * 5 + (P(), P("col", "row"), P("row", "col"), P("row", "col")),
        out_specs=(field, field, P("col", "row")),
        check_vma=False,
    )
```

time: 453 us -> 70.3 us (0.16); the launches traced: 447 us -> 70.2 us
  waiting for transfers between devices: 130 us -> 0 us
  starting transfers between devices: 106 us -> 0 us
  other arithmetic: 96.8 us -> 0 us
  blocking collectives: 66.3 us -> 0 us
  Pallas kernels: 0 us -> 65.6 us
  local copies, waits for them, and re-layouts: 32.4 us -> 3.87 us
  between operations: 15.7 us -> 0.65 us
    unnamed x2 -> x0, waiting for transfers between devices: 126 us -> none
    ppermute x32 -> x0, starting transfers between devices: 106 us -> none  [the longest x16 74.9 us: extended(): lax.ppermute(lax.slice_in_dim(block, block.shape[dim] - width, None, axis...]
    squeeze x1 -> x0, blocking collectives: 66.3 us -> none  [local(): slot_gamma = jnp.where(live, 0.25 * strip[0][safe_patch], jnp.float32(0.0))]
    pallas_call x0 -> x1, Pallas kernels: none -> 65.6 us  [local(): pl.pallas_call(kernel, out_shape=(jax.ShapeDtypeStruct(block, F32), jax.S...]
    scatter-add x2 -> x0, other arithmetic: 27.3 us -> none  [the longest x1 14.4 us: local(): jnp.zeros((c2.size,), jnp.float32).at[safe_cell].add(slot_gamma)]
    mul x4 -> x0, other arithmetic: 26.7 us -> none  [sweep(): m_new = m_low + 2.0 * weight + apply_laplace(c2 * weight)]
    gather x2 -> x0, local copies, waits for them, and re-layouts: 23.6 us -> none  [the longest x1 11.8 us: local(): slot_gamma = jnp.where(live, 0.25 * strip[0][safe_patch], jnp.float32(0.0))]
    div x3 -> x0, other arithmetic: 21.5 us -> none  [sweep(): states.append((drive - (1.0 - gamma) * prev) / (1.0 + gamma))]
  transfers between devices with their start and end apart: 33 -> 0, of which waited for: 2 -> 0; matrix products, arithmetic and copies ran while one was open for 24% -> 0% of each run, Pallas kernels for 0% -> 0%
where the time goes in v1:
time: 70.3 us; the launch traced here: 70.2 us
  Pallas kernels  65.6 us (93%)
  local copies, waits for them, and re-layouts  3.87 us (6%)
    pallas_call x1, Pallas kernels, local(): pl.pallas_call(kernel, out_shape=(jax.ShapeDtypeStruct(block, F32), jax.S...  65.6 us
    unnamed x7, local copies, waits for them, and re-layouts  3.87 us

profile of v1, /device:TPU:1, one launch (start us, length us, event | category | flops | bytes accessed | tf_op | source)
XLA Modules:
  0.0 70.2 jit_solution(11184181063894589150)
XLA Ops:
  0.6 65.6 %shard_map.112 = (f32[16,128,128]{2,1,0:T(8,128)}, f32[16,128,128]{2,1,0:T(8,128)}, f32[1,64]{1,0:T(1,128)}) custom-call(f32[16,128,128]{2,1,0:T(8,128)} %p0_in.1, f32[16,128,128]{2,1,0:T(8,128)} %p1_in.1, f32[16,128,128]{2,1,0:T(8,128)} %m4_in.1, f32[16,128,128]{2,1,0:T(8,128)} %m5_in.1, s32[16,128,128]{2,1,0:T(8,128)} %mat_in.1, f32[8]{0:T(128)} %speed.1, ...), custom_call_target="tpu_custom_call" | custom-call | tf_op jit(solution)/shard_map/pallas_call | solution.py:418
  66.3 0.0 copy-start
  66.3 2.4 %copy.15 = f32[16,128,128]{2,1,0:T(8,128)} copy(f32[16,128,128]{2,1,0:T(8,128)} %get-tuple-element.6) | data formatting | bytes 2097152
  68.7 0.0 copy-done
  68.7 0.0 copy-start.1
  68.7 1.0 %copy.16 = f32[16,128,128]{2,1,0:T(8,128)} copy(f32[16,128,128]{2,1,0:T(8,128)S(1)} %copy-done) | data formatting | bytes 2097152
  69.6 0.0 copy-done.1
  69.6 0.5 copy.17
Async XLA Ops:
  66.3 2.4 %copy-start = (f32[16,128,128]{2,1,0:T(8,128)S(1)}, f32[16,128,128]{2,1,0:T(8,128)}, u32[]{:S(2)}) copy-start(f32[16,128,128]{2,1,0:T(8,128)} %get-tuple-element.7) | copy-start | bytes 3145732
  68.7 1.0 %copy-start.1 = (f32[1,64]{1,0:T(1,128)S(1)}, f32[1,64]{1,0:T(1,128)}, u32[]{:S(2)}) copy-start(f32[1,64]{1,0:T(1,128)} %get-tuple-element.8) | copy-start | bytes 772

commit v2 on v1

v2 whole, which is shorter than its diff:
```python
import jax
import jax.numpy as jnp
from jax import lax
from jax.experimental import pallas as pl
from jax.experimental.pallas import tpu as pltpu
from jax.sharding import PartitionSpec as P

MESH = pl.DeviceIdType.MESH
F32 = jnp.float32
BF16 = jnp.bfloat16
CX, CY, NZ = 16, 128, 128
SLOTS = 2048
ROWS = 32
COLS = 8
SHARE = 64
PX, PY = CX + 2, CY + 16
GROUP = 7
EDGE = 14
PAIR = 7


def natural(step):
    return pl.ds(step, 8, 16)


def along(field, x, count, beside):
    value = field[pl.ds(x, count), 8 : 8 + CY, :].reshape(count * CY, NZ)
    high = value.astype(BF16)
    low = (value - high.astype(F32)).astype(BF16)
    return jnp.dot(
        jnp.concatenate([high, low], axis=1), beside[...], preferred_element_type=F32
    )


def around(field, x, tiles, sums):
    at = lambda plane, t: field[plane, pl.ds(8 + 8 * t, 8), :]
    line = {t: at(x, t) for t in range(tiles[0] - 1, tiles[-1] + 2)}
    found = []
    for t in tiles:
        here = line[t]
        total = (at(x - 1, t) + at(x + 1, t)) + (line[t - 1] + line[t + 1])
        found.append((t, here, total + sums(t) - 6.0 * here))
    return found


def put(field, x, t, value):
    field[x, pl.ds(8 + 8 * t, 8), :] = value
    if t == 15:
        field[x, 1:8, :] = value[0:7]
    if t == 0:
        field[x, CY + 8 : CY + 15, :] = value[1:8]


def kernel(
    p0_in, p1_in, m4_in, m5_in, mat_in, speed, adm, cell, patch,
    g0_out, g1_out, pg_out,
    kinds, raw_p1, raw_p0, raw_m5, raw_m4,
    f0, f1, f2, f3, f4, f5, f6, f7,
    c2, q, before, base0, base1, diff0, diff1, w0, w1, w2, w3, last,
    zs, beside, side, rt, bt, vt, gt, own, table, parts, arrived,
    load_sem, send_sem, recv_sem, share_sem,
):
    fields = (f0, f1, f2, f3, f4, f5, f6, f7)
    bases = (base0, base1)
    diffs = (diff0, diff1)
    weights = (w0, w1, w2, w3)
    row = lax.axis_index("row")
    col = lax.axis_index("col")

    pairs = (
        (p1_in, raw_p1), (mat_in, kinds), (p0_in, raw_p0), (m5_in, raw_m5), (m4_in, raw_m4)
    )
    loads = [
        pltpu.make_async_copy(ref, raw, load_sem.at[n]) for n, (ref, raw) in enumerate(pairs)
    ]
    for load in loads:
        load.start()

    barrier = pltpu.get_barrier_semaphore()

    def greet(step, carry):
        pl.semaphore_signal(
            barrier, inc=1, device_id=(lax.rem(row + step, ROWS), col), device_id_type=MESH
        )
        return carry

    lax.fori_loop(1, ROWS, greet, 0)
    for step in (1, COLS - 1):
        pl.semaphore_signal(
            barrier, inc=1, device_id=(row, lax.rem(col + step, COLS)), device_id_type=MESH
        )

    zero_plane = jnp.zeros((CY, NZ), F32)
    zero_row = jnp.zeros((CX, 1, NZ), F32)

    @pl.when(row == 0)
    def _():
        for f in range(8):
            fields[f][0, 8 : 8 + CY, :] = zero_plane

    @pl.when(row == ROWS - 1)
    def _():
        for f in range(8):
            fields[f][PX - 1, 8 : 8 + CY, :] = zero_plane

    @pl.when(col == 0)
    def _():
        for f in range(8):
            fields[f][1 : 1 + CX, 0:1, :] = zero_row

    @pl.when(col == COLS - 1)
    def _():
        for f in range(8):
            fields[f][1 : 1 + CX, PY - 1 : PY, :] = zero_row

    own[...] = jnp.zeros_like(own)
    own[0, :, 0:SHARE] = adm[...]
    table[pl.ds(row, 1)] = own[...]

    pl.semaphore_wait(barrier, ROWS + 1)

    sides = (
        (row < ROWS - 1, (row + 1, col)),
        (row > 0, (row - 1, col)),
        (col < COLS - 1, (row, col + 1)),
        (col > 0, (row, col - 1)),
    )
    comes = (row > 0, row < ROWS - 1, col > 0, col < COLS - 1)

    def copies(f):
        field = fields[f]
        pairs = (
            (field.at[CX, 8 : 8 + CY, :], field.at[0, 8 : 8 + CY, :]),
            (field.at[1, 8 : 8 + CY, :], field.at[PX - 1, 8 : 8 + CY, :]),
            (field.at[1 : 1 + CX, CY + 7 : CY + 8, :], field.at[1 : 1 + CX, 0:1, :]),
            (field.at[1 : 1 + CX, 8:9, :], field.at[1 : 1 + CX, PY - 1 : PY, :]),
        )
        if f == 0:
            pairs = (
                (p1_in.at[CX - 1], side.at[0]),
                (p1_in.at[0], side.at[1]),
                (p1_in.at[:, CY - 1 : CY, :], pairs[2][1]),
                (p1_in.at[:, 0:1, :], pairs[3][1]),
            )
        return [
            pltpu.make_async_remote_copy(
                src, dst, send_sem.at[f, d], recv_sem.at[f, d],
                device_id=sides[d][1], device_id_type=MESH,
            )
            for d, (src, dst) in enumerate(pairs)
        ]

    def send(f):
        for d, copy in enumerate(copies(f)):
            pl.when(sides[d][0])(copy.start)

    def receive(f):
        for d, copy in enumerate(copies(f)):
            pl.when(comes[d])(copy.wait_recv)

    def sent(f):
        for d, copy in enumerate(copies(f)):
            pl.when(sides[d][0])(copy.wait_send)

    send(0)

    def share(source, sem):
        def start(step, carry):
            to = lax.rem(row + step, ROWS)
            pltpu.make_async_remote_copy(
                source(to), (table if sem == 0 else arrived).at[pl.ds(row, 1)],
                share_sem.at[2 * sem], share_sem.at[2 * sem + 1],
                device_id=(to, col), device_id_type=MESH,
            ).start()
            return carry

        lax.fori_loop(1, ROWS, start, 0)

    def shared(buffer, which):
        rest = buffer.at[pl.ds(0, ROWS - 1)]
        pltpu.make_async_copy(rest, rest, share_sem.at[which]).wait()

    share(lambda to: own, 0)

    cells = cell[...]
    spots = patch[...]
    depth = cells & (NZ - 1)
    y = (cells >> 7) & (CY - 1)
    line = (cells >> 14) * CY + (y & 15) * 8 + (y >> 4)
    owner = spots >> 6
    place = spots & (SHARE - 1)

    def build(block, carry):
        start = pl.multiple_of(block * 16, 16)
        index = lax.broadcasted_iota(jnp.int32, (16, SLOTS), 0) + start
        rt[pl.ds(start, 16), :] = jnp.where(index == line, 1.0, 0.0).astype(BF16)
        return carry

    lax.fori_loop(0, SLOTS // 16, build, 0)
    index = lax.broadcasted_iota(jnp.int32, (2 * NZ, NZ), 0) & (NZ - 1)
    apart = index - lax.broadcasted_iota(jnp.int32, (2 * NZ, NZ), 1)
    beside[...] = jnp.where((apart == 1) | (apart == -1), 1.0, 0.0).astype(BF16)
    index = lax.broadcasted_iota(jnp.int32, (NZ, SLOTS), 0)
    bt[...] = jnp.where(index == place, 1.0, 0.0).astype(BF16)

    loads[0].wait()
    loads[1].wait()
    speeds = [speed[n] for n in range(8)]

    def arrange(x, carry):
        values = [raw_p1[x, natural(t), :] for t in range(16)]
        sorts = [kinds[x, natural(t), :] for t in range(16)]
        for t in range(16):
            put(f0, x + 1, t, values[t])
        for t in range(16):
            value = jnp.full((8, NZ), speeds[0], F32)
            for n in range(1, 8):
                value = jnp.where(sorts[t] == n, speeds[n], value)
            c2[x, pl.ds(8 * t, 8), :] = value
        return carry

    lax.fori_loop(0, CX, arrange, 0)

    loads[2].wait()
    loads[3].wait()
    loads[4].wait()

    def arrange_rest(x, carry):
        values = [raw_p0[x, natural(t), :] for t in range(16)]
        for t in range(16):
            before[x, pl.ds(8 * t, 8), :] = values[t]
        return carry

    lax.fori_loop(0, CX, arrange_rest, 0)

    shared(table, 1)
    shared(table, 0)
    strip = 0.25 * table[:, 0, :]
    strip_high = strip.astype(BF16)
    strip_low = (strip - strip_high.astype(F32)).astype(BF16)
    found = jnp.dot(
        jnp.concatenate([strip_high, strip_low], axis=0), bt[...], preferred_element_type=F32
    )
    found = found[:ROWS] + found[ROWS:]
    index = lax.broadcasted_iota(jnp.int32, (ROWS, SLOTS), 0)
    slot = jnp.sum(jnp.where(index == owner, found, 0.0), axis=0, keepdims=True)
    slot_high = slot.astype(BF16).astype(F32)
    slot_low = slot - slot_high
    index = lax.broadcasted_iota(jnp.int32, (NZ, SLOTS), 0)
    vt[0:NZ, :] = jnp.where(index == depth, slot_high, 0.0).astype(BF16)
    vt[NZ : 2 * NZ, :] = jnp.where(index == depth, slot_low, 0.0).astype(BF16)

    def spread(pair, carry):
        start = pl.multiple_of(pair * 256, 256)
        both = lax.dot_general(
            rt[pl.ds(start, 256), :], vt[...], (((1,), (1,)), ((), ())), preferred_element_type=F32
        )
        for half in range(2):
            x = 2 * pair + half
            for t in range(16):
                at = half * CY + 8 * t
                gamma = both[at : at + 8, 0:NZ] + both[at : at + 8, NZ : 2 * NZ]
                here = pl.ds(8 * t, 8)
                scale = 1.0 / (1.0 + gamma)
                high = raw_m5[x, natural(t), :]
                low = raw_m4[x, natural(t), :]
                weight = scale * high
                twice = 2.0 * weight
                q[x, here, :] = scale
                w0[x, here, :] = weight
                put(f4, x + 1, t, c2[x, here, :] * weight)
                base0[x, here, :] = low + twice
                diff0[x, here, :] = high - twice
        return carry

    lax.fori_loop(0, CX // 2, spread, 0, unroll=4)
    send(4)

    def forward(k):
        def group(work):
            found = []
            for x, tiles, sums in work:
                for t, here, change in around(fields[k - 1], x, tiles, sums):
                    at = pl.ds(8 * t, 8)
                    if k == 1:
                        old = before[x - 1, at, :]
                    else:
                        old = fields[k - 2][x, pl.ds(8 + 8 * t, 8), :]
                    new = old + q[x - 1, at, :] * (2.0 * (here - old) + c2[x - 1, at, :] * change)
                    found.append((x, t, new))
            for x, t, new in found:
                if k == 4:
                    last[x - 1, pl.ds(8 * t, 8), :] = new
                else:
                    put(fields[k], x, t, new)

        return fields[k - 1], group

    def adjoint(k):
        f = 8 - k
        base, next_base = bases[k % 2], bases[1 - k % 2]
        diff, next_diff = diffs[k % 2], diffs[1 - k % 2]

        def group(work):
            found = []
            for x, tiles, sums in work:
                for t, here, change in around(fields[f], x, tiles, sums):
                    at = pl.ds(8 * t, 8)
                    high = base[x - 1, at, :] + change
                    if k == 1:
                        found.append((x, t, high))
                        continue
                    weight = q[x - 1, at, :] * high
                    twice = 2.0 * weight
                    found.append(
                        (x, t, weight, c2[x - 1, at, :] * weight,
                         diff[x - 1, at, :] + twice, high - twice)
                    )
            for x, t, *values in found:
                at = pl.ds(8 * t, 8)
                if k == 1:
                    g1_out[x - 1, natural(t), :] = values[0]
                    continue
                weights[f - 3][x - 1, at, :] = values[0]
                put(fields[f + 1], x, t, values[1])
                next_base[x - 1, at, :] = values[2]
                if k == 2:
                    g0_out[x - 1, natural(t), :] = values[3]
                else:
                    next_diff[x - 1, at, :] = values[3]

        return fields[f], group

    def inside(step):
        field, group = step

        def body(n, carry):
            x = 2 + PAIR * n
            sums = along(field, x, PAIR, beside)
            for i in range(PAIR):
                tile = lambda t, i=i: sums[CY * i + 8 * t : CY * i + 8 * t + 8]
                for t in (0, 15):
                    zs[x + i - 1, pl.ds(8 * t, 8), :] = tile(t)
                for start in range(1, 15, GROUP):
                    group([(x + i, range(start, start + GROUP), tile)])
            return carry

        for x in (1, CX):
            zs[x - 1] = along(field, x, 1, beside)
        lax.fori_loop(0, 14 // PAIR, body, 0)

    def outside(step):
        field, group = step

        def tile(x):
            return lambda t: zs[x - 1, pl.ds(8 * t, 8), :]

        def ends(n, carry):
            x = 1 + n * (CX - 1)
            for start in range(0, 16, 8):
                group([(x, range(start, start + 8), tile(x))])
            return carry

        def edges(n, carry):
            x = 2 + EDGE * n
            for t in (0, 15):
                group([(x + i, (t,), tile(x + i)) for i in range(EDGE)])
            return carry

        lax.fori_loop(0, 2, ends, 0)
        lax.fori_loop(0, 14 // EDGE, edges, 0)

    inside(forward(1))
    receive(0)
    for n, plane, there in ((0, 0, comes[0]), (1, PX - 1, comes[1])):
        def place_side(n=n, plane=plane):
            for t in range(16):
                f0[plane, pl.ds(8 + 8 * t, 8), :] = side[n, natural(t), :]

        pl.when(there)(place_side)
    outside(forward(1))
    send(1)

    for k in (2, 3, 4):
        level = 6 - k
        step = adjoint(level)
        inside(step)
        receive(8 - level)
        outside(step)
        send(9 - level)
        step = forward(k)
        inside(step)
        receive(k - 1)
        outside(step)
        if k < 4:
            send(k)

    def collect(x, carry):
        tiles = []
        for t in range(16):
            at = pl.ds(8 * t, 8)
            inner = pl.ds(8 + 8 * t, 8)
            states = [before[x, at, :]]
            states += [fields[k][x + 1, inner, :] for k in range(4)]
            states.append(last[x, at, :])
            total = w3[x, at, :] * (states[0] - states[2])
            for k in (2, 3, 4):
                total = total + weights[4 - k][x, at, :] * (states[k - 1] - states[k + 1])
            tiles.append(0.25 * total)
        turned = jnp.concatenate(tiles, axis=0).T
        high = turned.astype(BF16)
        lane = pl.ds(pl.multiple_of(x * CY, CY), CY)
        gt[0:NZ, lane] = high
        gt[NZ : 2 * NZ, lane] = (turned - high.astype(F32)).astype(BF16)
        return carry

    lax.fori_loop(0, CX, collect, 0, unroll=4)
    total = jnp.zeros((2 * ROWS, NZ), F32)
    for chunk in range(SLOTS // 256):
        lanes = slice(256 * chunk, 256 * chunk + 256)
        picked = jnp.dot(gt[...], rt[:, lanes], preferred_element_type=F32)
        picked = picked[:NZ] + picked[NZ:]
        index = lax.broadcasted_iota(jnp.int32, (NZ, 256), 0)
        value = jnp.sum(
            jnp.where(index == depth[:, lanes], picked, 0.0), axis=0, keepdims=True
        )
        high = value.astype(BF16).astype(F32)
        low = value - high
        index = lax.broadcasted_iota(jnp.int32, (ROWS, 256), 0)
        mine = index == owner[:, lanes]
        both = jnp.concatenate(
            [jnp.where(mine, high, 0.0), jnp.where(mine, low, 0.0)], axis=0
        ).astype(BF16)
        total = total + lax.dot_general(
            both, bt[:, lanes], (((1,), (1,)), ((), ())), preferred_element_type=F32
        )
    parts[:, 0, :] = total[:ROWS] + total[ROWS:]
    arrived[pl.ds(row, 1)] = parts[pl.ds(row, 1)]
    share(lambda to: parts.at[pl.ds(to, 1)], 1)

    step = adjoint(1)
    inside(step)
    receive(7)
    outside(step)

    shared(arrived, 3)
    shared(arrived, 2)
    pg_out[...] = jnp.sum(arrived[...], axis=0)[:, 0:SHARE]
    for f in range(8):
        sent(f)


def hand_over(g0_in, g1_in, pg_in, g0_out, g1_out, pg_out, sem):
    pairs = ((g0_in, g0_out), (g1_in, g1_out), (pg_in, pg_out))
    copies = [pltpu.make_async_copy(src, dst, sem.at[n]) for n, (src, dst) in enumerate(pairs)]
    for copy in copies:
        copy.start()
    for copy in copies:
        copy.wait()


def local(p0, p1, m4, m5, material, speed_sq, admittance, bound_cell, bound_patch):
    block = (CX, CY, NZ)
    anywhere = pl.BlockSpec(memory_space=pl.ANY)
    far = pl.BlockSpec(memory_space=pltpu.HBM)
    vmem = pl.BlockSpec(memory_space=pltpu.VMEM)
    shapes = (
        jax.ShapeDtypeStruct(block, F32),
        jax.ShapeDtypeStruct(block, F32),
        jax.ShapeDtypeStruct((1, SHARE), F32),
    )
    results = pl.pallas_call(
        kernel,
        out_shape=shapes,
        in_specs=[far] * 5 + [pl.BlockSpec(memory_space=pltpu.SMEM)] + [vmem] * 3,
        out_specs=(vmem,) * 3,
        scratch_shapes=[pltpu.VMEM(block, jnp.int32)]
        + [pltpu.VMEM(block, F32)] * 4
        + [pltpu.VMEM((PX, PY, NZ), F32)] * 8
        + [pltpu.VMEM(block, F32)] * 12
        + [
            pltpu.VMEM(block, F32),
            pltpu.VMEM((2 * NZ, NZ), BF16),
            pltpu.VMEM((2, CY, NZ), F32),
            pltpu.VMEM((SLOTS, SLOTS), BF16),
            pltpu.VMEM((NZ, SLOTS), BF16),
            pltpu.VMEM((2 * NZ, SLOTS), BF16),
            pltpu.VMEM((2 * NZ, SLOTS), BF16),
            pltpu.VMEM((1, 1, NZ), F32),
            pltpu.VMEM((ROWS, 1, NZ), F32),
            pltpu.VMEM((ROWS, 1, NZ), F32),
            pltpu.VMEM((ROWS, 1, NZ), F32),
            pltpu.SemaphoreType.DMA((5,)),
            pltpu.SemaphoreType.DMA((8, 4)),
            pltpu.SemaphoreType.DMA((8, 4)),
            pltpu.SemaphoreType.DMA((4,)),
        ],
        compiler_params=pltpu.CompilerParams(
            collective_id=0, has_side_effects=True, vmem_limit_bytes=48 << 20
        ),
    )(p0, p1, m4, m5, material, speed_sq, admittance, bound_cell, bound_patch)
    return pl.pallas_call(
        hand_over,
        out_shape=shapes,
        in_specs=[vmem] * 3,
        out_specs=(anywhere,) * 3,
        scratch_shapes=[pltpu.SemaphoreType.DMA((3,))],
        compiler_params=pltpu.CompilerParams(vmem_limit_bytes=4 << 20),
    )(*results)


def solution(mesh):
    field = P("row", "col", None)
    return jax.shard_map(
        local,
        mesh=mesh,
        in_specs=(field,) * 5 + (P(), P("col", "row"), P("row", "col"), P("row", "col")),
        out_specs=(field, field, P("col", "row")),
        check_vma=False,
    )
```

time: 70.3 us -> 56.6 us (0.81)
  Pallas kernels: 65.6 us -> 49.2 us
  local copies, waits for them, and re-layouts: 3.87 us -> 6.37 us
    pallas_call x1 -> x2, Pallas kernels: 65.6 us -> 49.2 us  [the longest x1 47.9 us: local(): pl.pallas_call(kernel, out_shape=shapes, in_specs=[far] * 5 + [pl.BlockSp...]
    unnamed x7 -> x14, local copies, waits for them, and re-layouts: 3.87 us -> 6.37 us
where the time goes in v2:
time: 56.6 us; the launch traced here: 56.3 us
  Pallas kernels  49.2 us (87%)
  local copies, waits for them, and re-layouts  6.37 us (11%)
  between operations  0.66 us (1%)
    pallas_call x1, Pallas kernels, local(): pl.pallas_call(kernel, out_shape=shapes, in_specs=[far] * 5 + [pl.BlockSp...  47.9 us
    unnamed x14, local copies, waits for them, and re-layouts  6.37 us
    pallas_call x1, Pallas kernels, local(): pl.pallas_call(hand_over, out_shape=shapes, in_specs=[vmem] * 3, out_spec...  1.35 us

profile of v2, /device:TPU:1, one launch (start us, length us, event | category | flops | bytes accessed | tf_op | source)
XLA Modules:
  0.0 56.3 jit_solution(14034667075524236156)
XLA Ops:
  0.6 0.0 copy-start
  0.6 1.2 %copy-done = f32[16,128,128]{2,1,0:T(8,128)S(1)} copy-done((f32[16,128,128]{2,1,0:T(8,128)S(1)}, f32[16,128,128]{2,1,0:T(8,128)}, u32[]{:S(2)}) %copy-start) | copy-done | bytes 1048600
  1.9 0.0 copy-start.1
  1.9 1.2 %copy-done.1 = f32[16,128,128]{2,1,0:T(8,128)S(1)} copy-done((f32[16,128,128]{2,1,0:T(8,128)S(1)}, f32[16,128,128]{2,1,0:T(8,128)}, u32[]{:S(2)}) %copy-start.1) | copy-done | bytes 1048600
  3.1 0.0 copy-start.2
  3.1 1.2 %copy-done.2 = f32[16,128,128]{2,1,0:T(8,128)S(1)} copy-done((f32[16,128,128]{2,1,0:T(8,128)S(1)}, f32[16,128,128]{2,1,0:T(8,128)}, u32[]{:S(2)}) %copy-start.2) | copy-done | bytes 1048600
  4.3 0.0 copy-start.3
  4.3 0.7 %copy-done.3 = s32[1,2048]{1,0:T(1,128)S(1)} copy-done((s32[1,2048]{1,0:T(1,128)S(1)}, s32[1,2048]{1,0:T(1,128)}, u32[]{:S(2)}) %copy-start.3) | copy-done | bytes 8216
  5.0 0.0 copy-start.4
  5.0 0.7 %copy-done.4 = s32[1,2048]{1,0:T(1,128)S(1)} copy-done((s32[1,2048]{1,0:T(1,128)S(1)}, s32[1,2048]{1,0:T(1,128)}, u32[]{:S(2)}) %copy-start.4) | copy-done | bytes 8216
  5.7 0.0 copy-start.5
  5.7 0.7 %copy-done.5 = f32[8]{0:T(128)S(1)} copy-done((f32[8]{0:T(128)S(1)}, f32[8]{0:T(128)}, u32[]{:S(2)}) %copy-start.5) | copy-done | bytes 56
  6.4 0.0 copy-start.6
  6.4 0.7 %copy-done.6 = f32[1,64]{1,0:T(1,128)S(1)} copy-done((f32[1,64]{1,0:T(1,128)S(1)}, f32[1,64]{1,0:T(1,128)}, u32[]{:S(2)}) %copy-start.6) | copy-done | bytes 280
  7.0 47.9 %shard_map.112 = (f32[16,128,128]{2,1,0:T(8,128)S(1)}, f32[16,128,128]{2,1,0:T(8,128)S(1)}, f32[1,64]{1,0:T(1,128)S(1)}) custom-call(f32[16,128,128]{2,1,0:T(8,128)S(1)} %copy-done, f32[16,128,128]{2,1,0:T(8,128)S(1)} %copy-done.1, f32[16,128,128]{2,1,0:T(8,128)S(1)} %copy-done.2, f32[16,128,128]{2,1,0:T(8,128)} %m5_in.1, s32[16,128,128]{2,1,0:T(8,128)} %mat_in.1, ...), custom_call_target="tpu_custom_call" | custom-call | tf_op jit(solution)/shard_map/pallas_call | solution.py:472
  54.9 1.3 %shard_map.113 = (f32[16,128,128]{2,1,0:T(8,128)}, f32[16,128,128]{2,1,0:T(8,128)}, f32[1,64]{1,0:T(1,128)}) custom-call(f32[16,128,128]{2,1,0:T(8,128)S(1)} %get-tuple-element.6.g0_in, f32[16,128,128]{2,1,0:T(8,128)S(1)} %get-tuple-element.7.g1_in, f32[1,64]{1,0:T(1,128)S(1)} %get-tuple-element.8.pg_in), custom_call_target="tpu_custom_call" | custom-call | tf_op jit(solution)/shard_map/pallas_call | solution.py:502
Async XLA Ops:
  0.6 1.2 %copy-start = (f32[16,128,128]{2,1,0:T(8,128)S(1)}, f32[16,128,128]{2,1,0:T(8,128)}, u32[]{:S(2)}) copy-start(f32[16,128,128]{2,1,0:T(8,128)} %p0_in.1) | copy-start | bytes 3145732
  1.9 1.2 %copy-start.1 = (f32[16,128,128]{2,1,0:T(8,128)S(1)}, f32[16,128,128]{2,1,0:T(8,128)}, u32[]{:S(2)}) copy-start(f32[16,128,128]{2,1,0:T(8,128)} %p1_in.1) | copy-start | bytes 3145732
  3.1 1.2 %copy-start.2 = (f32[16,128,128]{2,1,0:T(8,128)S(1)}, f32[16,128,128]{2,1,0:T(8,128)}, u32[]{:S(2)}) copy-start(f32[16,128,128]{2,1,0:T(8,128)} %m4_in.1) | copy-start | bytes 3145732
  4.3 0.7 %copy-start.3 = (s32[1,2048]{1,0:T(1,128)S(1)}, s32[1,2048]{1,0:T(1,128)}, u32[]{:S(2)}) copy-start(s32[1,2048]{1,0:T(1,128)} %cell.1) | copy-start | bytes 24580
  5.0 0.7 %copy-start.4 = (s32[1,2048]{1,0:T(1,128)S(1)}, s32[1,2048]{1,0:T(1,128)}, u32[]{:S(2)}) copy-start(s32[1,2048]{1,0:T(1,128)} %patch.1) | copy-start | bytes 24580
  5.7 0.7 %copy-start.5 = (f32[8]{0:T(128)S(1)}, f32[8]{0:T(128)}, u32[]{:S(2)}) copy-start(f32[8]{0:T(128)} %speed.1) | copy-start | bytes 100
  6.4 0.7 %copy-start.6 = (f32[1,64]{1,0:T(1,128)S(1)}, f32[1,64]{1,0:T(1,128)}, u32[]{:S(2)}) copy-start(f32[1,64]{1,0:T(1,128)} %adm.1) | copy-start | bytes 772

commit v3 on v2

--- a/solution.py
+++ b/solution.py
@@ -17,6 +17,7 @@
 GROUP = 7
 EDGE = 14
 PAIR = 7
+RIM = 512
 
 
 def natural(step):
@@ -57,7 +58,7 @@
     kinds, raw_p1, raw_p0, raw_m5, raw_m4,
     f0, f1, f2, f3, f4, f5, f6, f7,
     c2, q, before, base0, base1, diff0, diff1, w0, w1, w2, w3, last,
-    zs, beside, side, rt, bt, vt, gt, own, table, parts, arrived,
+    zs, beside, side, rt, bt, vt, gt, rt_rim, gt_rim, own, table, parts, arrived,
     load_sem, send_sem, recv_sem, share_sem,
 ):
     fields = (f0, f1, f2, f3, f4, f5, f6, f7)
@@ -197,6 +198,20 @@
         return carry
 
     lax.fori_loop(0, SLOTS // 16, build, 0)
+    plane = cells >> 14
+    inner = jnp.where((y & 15) == 0, 256, 384) + 8 * (plane - 1) + (y >> 4)
+    inner = jnp.where(((y & 15) == 0) | ((y & 15) == 15), inner, -1)
+    ends_line = jnp.where(plane == 0, line, line - (CX - 2) * CY)
+    rim = jnp.where((plane == 0) | (plane == CX - 1), ends_line, inner)
+    rim = jnp.where(cells < 0, -1, rim)
+
+    def build_rim(block, carry):
+        start = pl.multiple_of(block * 16, 16)
+        index = lax.broadcasted_iota(jnp.int32, (16, SLOTS), 0) + start
+        rt_rim[pl.ds(start, 16), :] = jnp.where(index == rim, 1.0, 0.0).astype(BF16)
+        return carry
+
+    lax.fori_loop(0, RIM // 16, build_rim, 0)
     index = lax.broadcasted_iota(jnp.int32, (2 * NZ, NZ), 0) & (NZ - 1)
     apart = index - lax.broadcasted_iota(jnp.int32, (2 * NZ, NZ), 1)
     beside[...] = jnp.where((apart == 1) | (apart == -1), 1.0, 0.0).astype(BF16)
@@ -381,7 +396,7 @@
     outside(forward(1))
     send(1)
 
-    for k in (2, 3, 4):
+    for k in (2, 3):
         level = 6 - k
         step = adjoint(level)
         inside(step)
@@ -392,38 +407,65 @@
         inside(step)
         receive(k - 1)
         outside(step)
-        if k < 4:
-            send(k)
-
-    def collect(x, carry):
-        tiles = []
-        for t in range(16):
-            at = pl.ds(8 * t, 8)
-            inner = pl.ds(8 + 8 * t, 8)
-            states = [before[x, at, :]]
-            states += [fields[k][x + 1, inner, :] for k in range(4)]
-            states.append(last[x, at, :])
-            total = w3[x, at, :] * (states[0] - states[2])
-            for k in (2, 3, 4):
-                total = total + weights[4 - k][x, at, :] * (states[k - 1] - states[k + 1])
-            tiles.append(0.25 * total)
+        send(k)
+
+    def product(x, t):
+        at = pl.ds(8 * t, 8)
+        inner = pl.ds(8 + 8 * t, 8)
+        states = [before[x, at, :]]
+        states += [fields[k][x + 1, inner, :] for k in range(4)]
+        states.append(last[x, at, :])
+        total = w3[x, at, :] * (states[0] - states[2])
+        for k in (2, 3, 4):
+            total = total + weights[4 - k][x, at, :] * (states[k - 1] - states[k + 1])
+        return 0.25 * total
+
+    def turn(target, lane, tiles):
         turned = jnp.concatenate(tiles, axis=0).T
         high = turned.astype(BF16)
-        lane = pl.ds(pl.multiple_of(x * CY, CY), CY)
-        gt[0:NZ, lane] = high
-        gt[NZ : 2 * NZ, lane] = (turned - high.astype(F32)).astype(BF16)
-        return carry
-
-    lax.fori_loop(0, CX, collect, 0, unroll=4)
+        target[0:NZ, lane] = high
+        target[NZ : 2 * NZ, lane] = (turned - high.astype(F32)).astype(BF16)
+
+    def collect(x, carry):
+        none = jnp.zeros((8, NZ), F32)
+        tiles = [none] + [product(x, t) for t in range(1, 15)] + [none]
+        turn(gt, pl.ds(pl.multiple_of(x * CY, CY), CY), tiles)
+        return carry
+
+    def pick(source, start, stop, table_of_rows, lanes):
+        picked = jnp.dot(
+            source[:, start:stop], table_of_rows[start:stop, lanes], preferred_element_type=F32
+        )
+        picked = picked[:NZ] + picked[NZ:]
+        index = lax.broadcasted_iota(jnp.int32, (NZ, 256), 0)
+        return jnp.sum(
+            jnp.where(index == depth[:, lanes], picked, 0.0), axis=0, keepdims=True
+        )
+
+    step = adjoint(2)
+    ahead = forward(4)
+    inside(step)
+    receive(6)
+    outside(step)
+    send(7)
+    inside(ahead)
+    lax.fori_loop(1, CX - 1, collect, 0, unroll=2)
+    early = [
+        pick(gt, CY, (CX - 1) * CY, rt, slice(256 * c, 256 * c + 256))
+        for c in range(SLOTS // 256)
+    ]
+    receive(3)
+    outside(ahead)
+    none = jnp.zeros((8, NZ), F32)
+    turn(gt_rim, slice(0, CY), [product(0, t) for t in range(16)])
+    turn(gt_rim, slice(CY, 2 * CY), [product(CX - 1, t) for t in range(16)])
+    for n, t in ((2, 0), (3, 15)):
+        tiles = [product(x, t) for x in range(1, CX - 1)] + [none, none]
+        turn(gt_rim, slice(n * CY, (n + 1) * CY), tiles)
     total = jnp.zeros((2 * ROWS, NZ), F32)
     for chunk in range(SLOTS // 256):
         lanes = slice(256 * chunk, 256 * chunk + 256)
-        picked = jnp.dot(gt[...], rt[:, lanes], preferred_element_type=F32)
-        picked = picked[:NZ] + picked[NZ:]
-        index = lax.broadcasted_iota(jnp.int32, (NZ, 256), 0)
-        value = jnp.sum(
-            jnp.where(index == depth[:, lanes], picked, 0.0), axis=0, keepdims=True
-        )
+        value = early[chunk] + pick(gt_rim, 0, RIM, rt_rim, lanes)
         high = value.astype(BF16).astype(F32)
         low = value - high
         index = lax.broadcasted_iota(jnp.int32, (ROWS, 256), 0)
@@ -486,6 +528,8 @@
             pltpu.VMEM((NZ, SLOTS), BF16),
             pltpu.VMEM((2 * NZ, SLOTS), BF16),
             pltpu.VMEM((2 * NZ, SLOTS), BF16),
+            pltpu.VMEM((RIM, SLOTS), BF16),
+            pltpu.VMEM((2 * NZ, RIM), BF16),
             pltpu.VMEM((1, 1, NZ), F32),
             pltpu.VMEM((ROWS, 1, NZ), F32),
             pltpu.VMEM((ROWS, 1, NZ), F32),
@@ -496,7 +540,7 @@
             pltpu.SemaphoreType.DMA((4,)),
         ],
         compiler_params=pltpu.CompilerParams(
-            collective_id=0, has_side_effects=True, vmem_limit_bytes=48 << 20
+            collective_id=0, has_side_effects=True, vmem_limit_bytes=52400 << 10
         ),
     )(p0, p1, m4, m5, material, speed_sq, admittance, bound_cell, bound_patch)
     return pl.pallas_call(

time: 56.6 us -> 53.1 us (0.938)
  local copies, waits for them, and re-layouts: 6.37 us -> 2.7 us
    unnamed x14 -> x8, local copies, waits for them, and re-layouts: 6.37 us -> 2.7 us
where the time goes in v3:
time: 53.1 us; the launch traced here: 52.9 us
  Pallas kernels  49.6 us (93%)
  local copies, waits for them, and re-layouts  2.7 us (5%)
  between operations  0.65 us (1%)
    pallas_call x1, Pallas kernels, local(): pl.pallas_call(kernel, out_shape=shapes, in_specs=[far] * 5 + [pl.BlockSp...  48.2 us
    unnamed x8, local copies, waits for them, and re-layouts  2.7 us
    pallas_call x1, Pallas kernels, local(): pl.pallas_call(hand_over, out_shape=shapes, in_specs=[vmem] * 3, out_spec...  1.35 us

profile of v3, /device:TPU:1, one launch (start us, length us, event | category | flops | bytes accessed | tf_op | source)
XLA Modules:
  0.0 52.9 jit_solution(1728688521496307448)
XLA Ops:
  0.6 0.0 copy-start
  0.6 0.7 %copy-done = s32[1,2048]{1,0:T(1,128)S(1)} copy-done((s32[1,2048]{1,0:T(1,128)S(1)}, s32[1,2048]{1,0:T(1,128)}, u32[]{:S(2)}) %copy-start) | copy-done | bytes 8216
  1.3 0.0 copy-start.1
  1.3 0.7 %copy-done.1 = s32[1,2048]{1,0:T(1,128)S(1)} copy-done((s32[1,2048]{1,0:T(1,128)S(1)}, s32[1,2048]{1,0:T(1,128)}, u32[]{:S(2)}) %copy-start.1) | copy-done | bytes 8216
  2.0 0.0 copy-start.2
  2.0 0.7 %copy-done.2 = f32[8]{0:T(128)S(1)} copy-done((f32[8]{0:T(128)S(1)}, f32[8]{0:T(128)}, u32[]{:S(2)}) %copy-start.2) | copy-done | bytes 56
  2.7 0.0 copy-start.3
  2.7 0.7 %copy-done.3 = f32[1,64]{1,0:T(1,128)S(1)} copy-done((f32[1,64]{1,0:T(1,128)S(1)}, f32[1,64]{1,0:T(1,128)}, u32[]{:S(2)}) %copy-start.3) | copy-done | bytes 280
  3.3 48.2 %shard_map.112 = (f32[16,128,128]{2,1,0:T(8,128)S(1)}, f32[16,128,128]{2,1,0:T(8,128)S(1)}, f32[1,64]{1,0:T(1,128)S(1)}) custom-call(f32[16,128,128]{2,1,0:T(8,128)} %p0_in.1, f32[16,128,128]{2,1,0:T(8,128)} %p1_in.1, f32[16,128,128]{2,1,0:T(8,128)} %m4_in.1, f32[16,128,128]{2,1,0:T(8,128)} %m5_in.1, s32[16,128,128]{2,1,0:T(8,128)} %mat_in.1, ...), custom_call_target="tpu_custom_call" | custom-call | tf_op jit(solution)/shard_map/pallas_call | solution.py:514
  51.6 1.3 %shard_map.113 = (f32[16,128,128]{2,1,0:T(8,128)}, f32[16,128,128]{2,1,0:T(8,128)}, f32[1,64]{1,0:T(1,128)}) custom-call(f32[16,128,128]{2,1,0:T(8,128)S(1)} %get-tuple-element.6.g0_in, f32[16,128,128]{2,1,0:T(8,128)S(1)} %get-tuple-element.7.g1_in, f32[1,64]{1,0:T(1,128)S(1)} %get-tuple-element.8.pg_in), custom_call_target="tpu_custom_call" | custom-call | tf_op jit(solution)/shard_map/pallas_call | solution.py:546
Async XLA Ops:
  0.6 0.7 %copy-start = (s32[1,2048]{1,0:T(1,128)S(1)}, s32[1,2048]{1,0:T(1,128)}, u32[]{:S(2)}) copy-start(s32[1,2048]{1,0:T(1,128)} %cell.1) | copy-start | bytes 24580
  1.3 0.7 %copy-start.1 = (s32[1,2048]{1,0:T(1,128)S(1)}, s32[1,2048]{1,0:T(1,128)}, u32[]{:S(2)}) copy-start(s32[1,2048]{1,0:T(1,128)} %patch.1) | copy-start | bytes 24580
  2.0 0.7 %copy-start.2 = (f32[8]{0:T(128)S(1)}, f32[8]{0:T(128)}, u32[]{:S(2)}) copy-start(f32[8]{0:T(128)} %speed.1) | copy-start | bytes 100
  2.7 0.7 %copy-start.3 = (f32[1,64]{1,0:T(1,128)S(1)}, f32[1,64]{1,0:T(1,128)}, u32[]{:S(2)}) copy-start(f32[1,64]{1,0:T(1,128)} %adm.1) | copy-start | bytes 772

commit v4 on v3

--- a/solution.py
+++ b/solution.py
@@ -58,7 +58,7 @@
     kinds, raw_p1, raw_p0, raw_m5, raw_m4,
     f0, f1, f2, f3, f4, f5, f6, f7,
     c2, q, before, base0, base1, diff0, diff1, w0, w1, w2, w3, last,
-    zs, beside, side, rt, bt, vt, gt, rt_rim, gt_rim, own, table, parts, arrived,
+    zs, zs_last, beside, side, rt, bt, vt, gt, rt_rim, gt_rim, own, table, parts, arrived,
     load_sem, send_sem, recv_sem, share_sem,
 ):
     fields = (f0, f1, f2, f3, f4, f5, f6, f7)
@@ -309,7 +309,7 @@
                 else:
                     put(fields[k], x, t, new)
 
-        return fields[k - 1], group
+        return fields[k - 1], group, (zs_last if k == 4 else zs)
 
     def adjoint(k):
         f = 8 - k
@@ -344,10 +344,10 @@
                 else:
                     next_diff[x - 1, at, :] = values[3]
 
-        return fields[f], group
+        return fields[f], group, zs
 
     def inside(step):
-        field, group = step
+        field, group, kept = step
 
         def body(n, carry):
             x = 2 + PAIR * n
@@ -355,20 +355,20 @@
             for i in range(PAIR):
                 tile = lambda t, i=i: sums[CY * i + 8 * t : CY * i + 8 * t + 8]
                 for t in (0, 15):
-                    zs[x + i - 1, pl.ds(8 * t, 8), :] = tile(t)
+                    kept[x + i - 1, pl.ds(8 * t, 8), :] = tile(t)
                 for start in range(1, 15, GROUP):
                     group([(x + i, range(start, start + GROUP), tile)])
             return carry
 
         for x in (1, CX):
-            zs[x - 1] = along(field, x, 1, beside)
+            kept[x - 1] = along(field, x, 1, beside)
         lax.fori_loop(0, 14 // PAIR, body, 0)
 
     def outside(step):
-        field, group = step
+        field, group, kept = step
 
         def tile(x):
-            return lambda t: zs[x - 1, pl.ds(8 * t, 8), :]
+            return lambda t: kept[x - 1, pl.ds(8 * t, 8), :]
 
         def ends(n, carry):
             x = 1 + n * (CX - 1)
@@ -445,15 +445,15 @@
     step = adjoint(2)
     ahead = forward(4)
     inside(step)
-    receive(6)
-    outside(step)
-    send(7)
     inside(ahead)
     lax.fori_loop(1, CX - 1, collect, 0, unroll=2)
     early = [
         pick(gt, CY, (CX - 1) * CY, rt, slice(256 * c, 256 * c + 256))
         for c in range(SLOTS // 256)
     ]
+    receive(6)
+    outside(step)
+    send(7)
     receive(3)
     outside(ahead)
     none = jnp.zeros((8, NZ), F32)
@@ -521,6 +521,7 @@
         + [pltpu.VMEM((PX, PY, NZ), F32)] * 8
         + [pltpu.VMEM(block, F32)] * 12
         + [
+            pltpu.VMEM(block, F32),
             pltpu.VMEM(block, F32),
             pltpu.VMEM((2 * NZ, NZ), BF16),
             pltpu.VMEM((2, CY, NZ), F32),

time: 53.1 us -> 50.8 us (0.957)
  Pallas kernels: 49.6 us -> 47.3 us
    pallas_call x1, Pallas kernels: 48.2 us -> 45.9 us  [local(): pl.pallas_call(kernel, out_shape=shapes, in_specs=[far] * 5 + [pl.BlockSp...]
where the time goes in v4:
time: 50.8 us; the launch traced here: 50.6 us
  Pallas kernels  47.3 us (93%)
  local copies, waits for them, and re-layouts  2.7 us (5%)
  between operations  0.65 us (1%)
    pallas_call x1, Pallas kernels, local(): pl.pallas_call(kernel, out_shape=shapes, in_specs=[far] * 5 + [pl.BlockSp...  45.9 us
    unnamed x8, local copies, waits for them, and re-layouts  2.7 us
    pallas_call x1, Pallas kernels, local(): pl.pallas_call(hand_over, out_shape=shapes, in_specs=[vmem] * 3, out_spec...  1.35 us

profile of v4, /device:TPU:1, one launch (start us, length us, event | category | flops | bytes accessed | tf_op | source)
XLA Modules:
  0.0 50.6 jit_solution(13313297788384243654)
XLA Ops:
  0.6 0.0 copy-start
  0.6 0.7 %copy-done = s32[1,2048]{1,0:T(1,128)S(1)} copy-done((s32[1,2048]{1,0:T(1,128)S(1)}, s32[1,2048]{1,0:T(1,128)}, u32[]{:S(2)}) %copy-start) | copy-done | bytes 8216
  1.3 0.0 copy-start.1
  1.3 0.7 %copy-done.1 = s32[1,2048]{1,0:T(1,128)S(1)} copy-done((s32[1,2048]{1,0:T(1,128)S(1)}, s32[1,2048]{1,0:T(1,128)}, u32[]{:S(2)}) %copy-start.1) | copy-done | bytes 8216
  2.0 0.0 copy-start.2
  2.0 0.7 %copy-done.2 = f32[8]{0:T(128)S(1)} copy-done((f32[8]{0:T(128)S(1)}, f32[8]{0:T(128)}, u32[]{:S(2)}) %copy-start.2) | copy-done | bytes 56
  2.7 0.0 copy-start.3
  2.7 0.7 %copy-done.3 = f32[1,64]{1,0:T(1,128)S(1)} copy-done((f32[1,64]{1,0:T(1,128)S(1)}, f32[1,64]{1,0:T(1,128)}, u32[]{:S(2)}) %copy-start.3) | copy-done | bytes 280
  3.3 45.9 %shard_map.112 = (f32[16,128,128]{2,1,0:T(8,128)S(1)}, f32[16,128,128]{2,1,0:T(8,128)S(1)}, f32[1,64]{1,0:T(1,128)S(1)}) custom-call(f32[16,128,128]{2,1,0:T(8,128)} %p0_in.1, f32[16,128,128]{2,1,0:T(8,128)} %p1_in.1, f32[16,128,128]{2,1,0:T(8,128)} %m4_in.1, f32[16,128,128]{2,1,0:T(8,128)} %m5_in.1, s32[16,128,128]{2,1,0:T(8,128)} %mat_in.1, ...), custom_call_target="tpu_custom_call" | custom-call | tf_op jit(solution)/shard_map/pallas_call | solution.py:514
  49.3 1.3 %shard_map.113 = (f32[16,128,128]{2,1,0:T(8,128)}, f32[16,128,128]{2,1,0:T(8,128)}, f32[1,64]{1,0:T(1,128)}) custom-call(f32[16,128,128]{2,1,0:T(8,128)S(1)} %get-tuple-element.6.g0_in, f32[16,128,128]{2,1,0:T(8,128)S(1)} %get-tuple-element.7.g1_in, f32[1,64]{1,0:T(1,128)S(1)} %get-tuple-element.8.pg_in), custom_call_target="tpu_custom_call" | custom-call | tf_op jit(solution)/shard_map/pallas_call | solution.py:547
Async XLA Ops:
  0.6 0.7 %copy-start = (s32[1,2048]{1,0:T(1,128)S(1)}, s32[1,2048]{1,0:T(1,128)}, u32[]{:S(2)}) copy-start(s32[1,2048]{1,0:T(1,128)} %cell.1) | copy-start | bytes 24580
  1.3 0.7 %copy-start.1 = (s32[1,2048]{1,0:T(1,128)S(1)}, s32[1,2048]{1,0:T(1,128)}, u32[]{:S(2)}) copy-start(s32[1,2048]{1,0:T(1,128)} %patch.1) | copy-start | bytes 24580
  2.0 0.7 %copy-start.2 = (f32[8]{0:T(128)S(1)}, f32[8]{0:T(128)}, u32[]{:S(2)}) copy-start(f32[8]{0:T(128)} %speed.1) | copy-start | bytes 100
  2.7 0.7 %copy-start.3 = (f32[1,64]{1,0:T(1,128)S(1)}, f32[1,64]{1,0:T(1,128)}, u32[]{:S(2)}) copy-start(f32[1,64]{1,0:T(1,128)} %adm.1) | copy-start | bytes 772
